TPU v7x, 32 devices: a whole 2x2x4 slice. The times are simulated.
32 devices in a mesh: ctx: 8 (over z, core), head: 4 (over y, x).
Axes of the slice: x: 2, y: 2, z: 4, core: 2. Of those that a mesh axis runs over, the one named last changes fastest.
Arguments:
- query_states: bfloat16 [16384, 16, 128], P('ctx', 'head'), may hold values from -36 to 36, as said below
- key_states: bfloat16 [16384, 16, 128], P('ctx', 'head'), may hold values from -6 to 6
- value_states: bfloat16 [16384, 16, 128], P('ctx', 'head'), may hold values from -6 to 6
- block_pattern: int32 [16, 128, 128], P('head'), may hold values 0 or 1
- helper_distances: int32 [2], replicated, may hold values from 1 to 4, as said below
- out_weight: bfloat16 [16, 128, 4096], P('head'), may hold values from -0.125 to 0.125
Outputs:
- layer_output: bfloat16 [16384, 4096], P(('ctx', 'head'))
Inputs may be any that keep to these rules, and one draw needn't show every extreme that they name: `query_states`: Queries; some rows may be large multiples of key rows. `helper_distances`: the two distances differ, and one of them is always 8.
All inputs are finite; a program needn't handle non-finite values. No bound on the sum of `block_pattern` on one device may be relied on, other than what follows from the above.
Results may differ from a plain program's by a relative error of at most 0.015.
Values may be sent and summed in bfloat16 or wider, within the bound.
No kernel may reach another device: no remote copies, remote signals or barrier semaphores. Data moves between devices by JAX's collectives and lax.ppermute only.
A program may use at most 128 MiB of HBM per device.

v0:
```python
import jax
import jax.numpy as jnp
from jax import lax
from jax.sharding import PartitionSpec as P

BLOCK = 128


NEG_FILL = -1e30


def as_sent(array):
    return jax.tree.map(lambda a: a.astype(jnp.bfloat16) if a.dtype == jnp.float32 else a, array)


def from_behind(value, axis, steps):
    count = lax.axis_size(axis)
    first, last = (max(0, -steps), min(count, count - steps))
    return lax.ppermute(value, axis, [(source, source + steps) for source in range(first, last)])


def attend_source(query_part, key_part, value_part, pattern_rows, is_local):
    row_count = query_part.shape[0]
    key_count = key_part.shape[0]
    row_step = min(512, row_count)
    score_scale = query_part.shape[2] ** (-0.5)
    key_place = jnp.arange(key_count, dtype=jnp.int32)

    def one_block(block_number):
        first_row = block_number * row_step
        query_rows = lax.dynamic_slice_in_dim(query_part, first_row, row_step, 0)
        pattern_part = lax.dynamic_slice_in_dim(
            pattern_rows, first_row // BLOCK, row_step // BLOCK, 1
        )
        allowed = jnp.repeat(jnp.repeat(pattern_part > 0, BLOCK, axis=1), BLOCK, axis=2)
        if is_local:
            query_place = first_row + jnp.arange(row_step, dtype=jnp.int32)
            query_block = query_place // BLOCK
            key_block = key_place // BLOCK
            earlier = key_block[None, :] < query_block[:, None]
            same_block = (key_block[None, :] == query_block[:, None]) & (
                key_place[None, :] <= query_place[:, None]
            )
            allowed = allowed & earlier[None] | same_block[None]
        scores = (
            jnp.einsum("qhe,khe->hqk", query_rows, key_part, preferred_element_type=jnp.float32)
            * score_scale
        )
        masked = jnp.where(allowed, scores, NEG_FILL)
        row_peak = jnp.max(masked, axis=2)
        weights = jnp.where(allowed, jnp.exp(masked - row_peak[:, :, None]), 0.0)
        row_total = jnp.sum(weights, axis=2)
        numerator = jnp.einsum(
            "hqk,khe->qhe",
            weights.astype(jnp.bfloat16),
            value_part,
            preferred_element_type=jnp.float32,
        )
        return (numerator, row_peak.T, row_total.T)

    numerator, row_peak, row_total = lax.map(
        one_block, jnp.arange(row_count // row_step, dtype=jnp.int32)
    )
    heads_here = query_part.shape[1]
    return (
        numerator.reshape(row_count, heads_here, query_part.shape[2]),
        row_peak.reshape(row_count, heads_here),
        row_total.reshape(row_count, heads_here),
    )


def keep_valid(piece, is_valid):
    numerator, row_peak, row_total = piece
    return (
        jnp.where(is_valid, numerator, 0.0),
        jnp.where(is_valid, row_peak, NEG_FILL),
        jnp.where(is_valid, row_total, 0.0),
    )


def combine_sources(pieces):
    peak_score = pieces[0][1]
    for piece in pieces[1:]:
        peak_score = jnp.maximum(peak_score, piece[1])
    numerator_sum = jnp.zeros_like(pieces[0][0])
    denominator = jnp.zeros_like(pieces[0][1])
    for numerator, row_peak, row_total in pieces:
        factor = jnp.exp(row_peak - peak_score)
        numerator_sum = numerator_sum + factor[:, :, None] * numerator
        denominator = denominator + factor * row_total
    return (numerator_sum / denominator[:, :, None]).astype(jnp.bfloat16)


def bit_on(hop_count, bit_number):
    return hop_count // (1 << bit_number) % 2 == 1


def pick_moved(payload, shifted, hop_counts, bit_number):
    return tuple(
        (
            jnp.where(bit_on(hop_count, bit_number), after, before)
            for before, after, hop_count in zip(payload, shifted, hop_counts)
        )
    )


def send_pairs(payload, hop_counts):
    levels = lax.axis_size("ctx").bit_length() - 1
    for bit_number in range(levels):
        shifted = jax.tree.map(
            lambda part, own: part.astype(own.dtype),
            from_behind(as_sent(payload), "ctx", 1 << bit_number),
            payload,
        )
        payload = pick_moved(payload, shifted, hop_counts, bit_number)
    return payload


def pattern_slice(block_pattern, query_shard, key_shard, per_shard):
    starts = (jnp.zeros((), jnp.int32), query_shard * per_shard, key_shard * per_shard)
    return lax.dynamic_slice(block_pattern, starts, (block_pattern.shape[0], per_shard, per_shard))


def per_device(query_states, key_states, value_states, block_pattern, helper_distances, out_weight):
    my_shard = lax.axis_index("ctx")
    row_count = query_states.shape[0]
    per_shard = row_count // BLOCK
    pieces = [
        attend_source(
            query_states,
            key_states,
            value_states,
            pattern_slice(block_pattern, my_shard, my_shard, per_shard),
            True,
        )
    ]
    distance_set = (helper_distances[0], helper_distances[1])
    arrived = [
        send_pairs((key_states, value_states), (hop_count, hop_count)) for hop_count in distance_set
    ]
    for (far_keys, far_values), hop_count in zip(arrived, distance_set):
        source = my_shard - hop_count
        safe_source = jnp.maximum(source, 0)
        piece = attend_source(
            query_states,
            far_keys,
            far_values,
            pattern_slice(block_pattern, my_shard, safe_source, per_shard),
            False,
        )
        pieces.append(keep_valid(piece, source >= 0))
    attended = combine_sources(pieces)
    flattened = attended.reshape(row_count, attended.shape[1] * attended.shape[2])
    weight_rows = out_weight.reshape(out_weight.shape[0] * out_weight.shape[1], out_weight.shape[2])
    return lax.psum_scatter(
        jnp.dot(flattened, weight_rows, preferred_element_type=jnp.float32).astype(jnp.bfloat16),
        "head",
        scatter_dimension=0,
        tiled=True,
    )


def solution(mesh):
    placed = (
        P("ctx", "head", None),
        P("ctx", "head", None),
        P("ctx", "head", None),
        P("head", None, None),
        P(),
        P("head", None, None),
    )
    return jax.shard_map(
        per_device, mesh=mesh, in_specs=placed, out_specs=P(("ctx", "head"), None), check_vma=False
    )
```

profile of v0, /device:TPU:0, one launch (start us, length us, event | category | flops | bytes accessed | tf_op | source)
XLA Modules:
  0.0 1116.6 jit_solution(8749854801851948992)
XLA Ops:
  28.3 19.4 %collective-permute-start.4 = (bf16[2048,4,128]{2,0,1:T(8,128)(2,1)S(1)}, bf16[2048,4,128]{2,0,1:T(8,128)(2,1)}, u32[]{:S(2)}, u32[]{:S(2)}) collective-permute-start(bf16[2048,4,128]{2,0,1:T(8,128)(2,1)S(1)} %get-tuple-element.616), channel_id=1, source_target_pairs={{0,8},{4,12},{8,16},{12,20},{16,24},{20,28},{1,9},{5,13},{9,17},{1... | collective-permute-start | bytes 6291464 | tf_op jit(solution)/shard_map/ppermute | solution.py:19
  51.8 31.4 %collective-permute-start.1 = (bf16[2048,4,128]{2,0,1:T(8,128)(2,1)}, bf16[2048,4,128]{2,0,1:T(8,128)(2,1)}, u32[]{:S(2)}, u32[]{:S(2)}) collective-permute-start(bf16[2048,4,128]{2,0,1:T(8,128)(2,1)} %get-tuple-element.618), channel_id=1, source_target_pairs={{0,8},{4,12},{8,16},{12,20},{16,24},{20,28},{1,9},{5,13},{9,17},{1... | collective-permute-start | bytes 6291464 | tf_op jit(solution)/shard_map/ppermute | solution.py:19
  102.8 34.7 %collective-permute-done.1 = bf16[2048,4,128]{2,0,1:T(8,128)(2,1)} collective-permute-done((bf16[2048,4,128]{2,0,1:T(8,128)(2,1)}, bf16[2048,4,128]{2,0,1:T(8,128)(2,1)}, u32[]{:S(2)}, u32[]{:S(2)}) %collective-permute-start.1) | collective-permute-done | bytes 2097184 | tf_op jit(solution)/shard_map/ppermute | solution.py:19
  151.6 237.0 %while.53 = (s32[]{:T(128)}, f32[4,512,4,128]{3,1,0,2:T(8,128)}, f32[4,512,4]{1,2,0:T(4,128)}, f32[4,512,4]{1,2,0:T(4,128)}, s32[4]{0:T(128)}, /*index=5*/s32[4,...) while((s32[]{:T(128)}, f32[4,512,4,128]{3,1,0,2:T(8,128)}, ...), condition=%wide.region_3.4_spmd.clone.clone, body=%wide.region_0.3_spmd.clone.clone.sunk | while | flops 2231390976 | bytes 110787536 | solution.py:61
  153.5 16.0 %broadcast_in_dim.264 = pred[4,512,16,128]{3,2,1,0:T(8,128)(4,1)} broadcast(pred[4,512,16]{2,1,0:T(8,128)(4,1)S(1)} %bitcast.133), dimensions={0,1,2} | broadcast | bytes 4227072 | tf_op jit(solution)/shard_map/while/body/eval_jaxpr/broadcast_in_dim | solution.py:35
  169.6 12.0 %reshape.324 = pred[4,512,2048]{2,1,0:T(32,128)(4,1)} reshape(pred[4,512,16,128]{3,2,1,0:T(8,128)(4,1)} %broadcast_in_dim.264) | data formatting | bytes 8388608 | tf_op jit(solution)/shard_map/while/body/eval_jaxpr/reshape | solution.py:35
  212.8 16.0 %broadcast_in_dim.264 = pred[4,512,16,128]{3,2,1,0:T(8,128)(4,1)} broadcast(pred[4,512,16]{2,1,0:T(8,128)(4,1)S(1)} %bitcast.133), dimensions={0,1,2} | broadcast | bytes 4227072 | tf_op jit(solution)/shard_map/while/body/eval_jaxpr/broadcast_in_dim | solution.py:35
  228.8 12.0 %reshape.324 = pred[4,512,2048]{2,1,0:T(32,128)(4,1)} reshape(pred[4,512,16,128]{3,2,1,0:T(8,128)(4,1)} %broadcast_in_dim.264) | data formatting | bytes 8388608 | tf_op jit(solution)/shard_map/while/body/eval_jaxpr/reshape | solution.py:35
  272.0 16.0 %broadcast_in_dim.264 = pred[4,512,16,128]{3,2,1,0:T(8,128)(4,1)} broadcast(pred[4,512,16]{2,1,0:T(8,128)(4,1)S(1)} %bitcast.133), dimensions={0,1,2} | broadcast | bytes 4227072 | tf_op jit(solution)/shard_map/while/body/eval_jaxpr/broadcast_in_dim | solution.py:35
  288.1 12.0 %reshape.324 = pred[4,512,2048]{2,1,0:T(32,128)(4,1)} reshape(pred[4,512,16,128]{3,2,1,0:T(8,128)(4,1)} %broadcast_in_dim.264) | data formatting | bytes 8388608 | tf_op jit(solution)/shard_map/while/body/eval_jaxpr/reshape | solution.py:35
  331.3 16.0 %broadcast_in_dim.264 = pred[4,512,16,128]{3,2,1,0:T(8,128)(4,1)} broadcast(pred[4,512,16]{2,1,0:T(8,128)(4,1)S(1)} %bitcast.133), dimensions={0,1,2} | broadcast | bytes 4227072 | tf_op jit(solution)/shard_map/while/body/eval_jaxpr/broadcast_in_dim | solution.py:35
  347.3 12.0 %reshape.324 = pred[4,512,2048]{2,1,0:T(32,128)(4,1)} reshape(pred[4,512,16,128]{3,2,1,0:T(8,128)(4,1)} %broadcast_in_dim.264) | data formatting | bytes 8388608 | tf_op jit(solution)/shard_map/while/body/eval_jaxpr/reshape | solution.py:35
  409.8 196.9 %while.51 = (s32[]{:T(128)}, f32[4,512,4,128]{3,1,0,2:T(8,128)}, f32[4,512,4]{1,2,0:T(4,128)S(1)}, f32[4,512,4]{1,2,0:T(4,128)S(1)}, s32[4]{0:T(128)S(1)}, /*ind...) while((s32[]{:T(128)}, f32[4,512,4,128]{3,1,0,2:T(8,128)}, ...), condition=%wide.region_7.8_spmd, body=%wide.region_4.7_spmd.sunk | while | flops 2202005760 | bytes 98175408 | solution.py:61
  411.9 16.0 %broadcast_in_dim.250 = pred[4,512,16,128]{3,2,1,0:T(8,128)(4,1)} broadcast(pred[4,512,16]{2,1,0:T(8,128)(4,1)S(1)} %bitcast.134), dimensions={0,1,2} | broadcast | bytes 4227072 | tf_op jit(solution)/shard_map/while/body/eval_jaxpr/broadcast_in_dim | solution.py:35
  428.0 12.0 %reshape.322 = pred[4,512,2048]{2,1,0:T(32,128)(4,1)} reshape(pred[4,512,16,128]{3,2,1,0:T(8,128)(4,1)} %broadcast_in_dim.250) | data formatting | bytes 8388608 | tf_op jit(solution)/shard_map/while/body/eval_jaxpr/reshape | solution.py:35
  461.2 16.0 %broadcast_in_dim.250 = pred[4,512,16,128]{3,2,1,0:T(8,128)(4,1)} broadcast(pred[4,512,16]{2,1,0:T(8,128)(4,1)S(1)} %bitcast.134), dimensions={0,1,2} | broadcast | bytes 4227072 | tf_op jit(solution)/shard_map/while/body/eval_jaxpr/broadcast_in_dim | solution.py:35
  477.2 12.0 %reshape.322 = pred[4,512,2048]{2,1,0:T(32,128)(4,1)} reshape(pred[4,512,16,128]{3,2,1,0:T(8,128)(4,1)} %broadcast_in_dim.250) | data formatting | bytes 8388608 | tf_op jit(solution)/shard_map/while/body/eval_jaxpr/reshape | solution.py:35
  510.4 16.0 %broadcast_in_dim.250 = pred[4,512,16,128]{3,2,1,0:T(8,128)(4,1)} broadcast(pred[4,512,16]{2,1,0:T(8,128)(4,1)S(1)} %bitcast.134), dimensions={0,1,2} | broadcast | bytes 4227072 | tf_op jit(solution)/shard_map/while/body/eval_jaxpr/broadcast_in_dim | solution.py:35
  526.4 12.0 %reshape.322 = pred[4,512,2048]{2,1,0:T(32,128)(4,1)} reshape(pred[4,512,16,128]{3,2,1,0:T(8,128)(4,1)} %broadcast_in_dim.250) | data formatting | bytes 8388608 | tf_op jit(solution)/shard_map/while/body/eval_jaxpr/reshape | solution.py:35
  559.6 16.0 %broadcast_in_dim.250 = pred[4,512,16,128]{3,2,1,0:T(8,128)(4,1)} broadcast(pred[4,512,16]{2,1,0:T(8,128)(4,1)S(1)} %bitcast.134), dimensions={0,1,2} | broadcast | bytes 4227072 | tf_op jit(solution)/shard_map/while/body/eval_jaxpr/broadcast_in_dim | solution.py:35
  575.7 12.0 %reshape.322 = pred[4,512,2048]{2,1,0:T(32,128)(4,1)} reshape(pred[4,512,16,128]{3,2,1,0:T(8,128)(4,1)} %broadcast_in_dim.250) | data formatting | bytes 8388608 | tf_op jit(solution)/shard_map/while/body/eval_jaxpr/reshape | solution.py:35
  615.6 197.2 %while.52 = (s32[]{:T(128)}, f32[4,512,4,128]{3,1,0,2:T(8,128)}, f32[4,512,4]{1,2,0:T(4,128)S(1)}, f32[4,512,4]{1,2,0:T(4,128)S(1)}, s32[4]{0:T(128)S(1)}, /*ind...) while((s32[]{:T(128)}, f32[4,512,4,128]{3,1,0,2:T(8,128)}, ...), condition=%wide.region_11.12_spmd, body=%wide.region_8.11_spmd.sunk | while | flops 2202005760 | bytes 98175408 | solution.py:61
  618.0 16.1 %broadcast_in_dim.257 = pred[4,512,16,128]{3,2,1,0:T(8,128)(4,1)} broadcast(pred[4,512,16]{2,1,0:T(8,128)(4,1)S(1)} %bitcast.135), dimensions={0,1,2} | broadcast | bytes 4227072 | tf_op jit(solution)/shard_map/while/body/eval_jaxpr/broadcast_in_dim | solution.py:35
  634.1 12.0 %reshape.323 = pred[4,512,2048]{2,1,0:T(32,128)(4,1)} reshape(pred[4,512,16,128]{3,2,1,0:T(8,128)(4,1)} %broadcast_in_dim.257) | data formatting | bytes 8388608 | tf_op jit(solution)/shard_map/while/body/eval_jaxpr/reshape | solution.py:35
  667.3 16.1 %broadcast_in_dim.257 = pred[4,512,16,128]{3,2,1,0:T(8,128)(4,1)} broadcast(pred[4,512,16]{2,1,0:T(8,128)(4,1)S(1)} %bitcast.135), dimensions={0,1,2} | broadcast | bytes 4227072 | tf_op jit(solution)/shard_map/while/body/eval_jaxpr/broadcast_in_dim | solution.py:35
  683.3 12.0 %reshape.323 = pred[4,512,2048]{2,1,0:T(32,128)(4,1)} reshape(pred[4,512,16,128]{3,2,1,0:T(8,128)(4,1)} %broadcast_in_dim.257) | data formatting | bytes 8388608 | tf_op jit(solution)/shard_map/while/body/eval_jaxpr/reshape | solution.py:35
  716.5 16.1 %broadcast_in_dim.257 = pred[4,512,16,128]{3,2,1,0:T(8,128)(4,1)} broadcast(pred[4,512,16]{2,1,0:T(8,128)(4,1)S(1)} %bitcast.135), dimensions={0,1,2} | broadcast | bytes 4227072 | tf_op jit(solution)/shard_map/while/body/eval_jaxpr/broadcast_in_dim | solution.py:35
  732.6 12.0 %reshape.323 = pred[4,512,2048]{2,1,0:T(32,128)(4,1)} reshape(pred[4,512,16,128]{3,2,1,0:T(8,128)(4,1)} %broadcast_in_dim.257) | data formatting | bytes 8388608 | tf_op jit(solution)/shard_map/while/body/eval_jaxpr/reshape | solution.py:35
  765.7 16.1 %broadcast_in_dim.257 = pred[4,512,16,128]{3,2,1,0:T(8,128)(4,1)} broadcast(pred[4,512,16]{2,1,0:T(8,128)(4,1)S(1)} %bitcast.135), dimensions={0,1,2} | broadcast | bytes 4227072 | tf_op jit(solution)/shard_map/while/body/eval_jaxpr/broadcast_in_dim | solution.py:35
  781.8 12.0 %reshape.323 = pred[4,512,2048]{2,1,0:T(32,128)(4,1)} reshape(pred[4,512,16,128]{3,2,1,0:T(8,128)(4,1)} %broadcast_in_dim.257) | data formatting | bytes 8388608 | tf_op jit(solution)/shard_map/while/body/eval_jaxpr/reshape | solution.py:35
  821.0 11.4 %bitcast_convert_fusion = bf16[2048,4096]{1,0:T(8,128)(2,1)} fusion(bf16[2048,4,128]{2,0,1:T(8,128)(2,1)S(1)} %fusion.65, bf16[4,128,4096]{2,1,0:T(8,128)(2,1)S(1)} %copy-done.14), kind=kOutput, calls=%fused_computation.73 | convolution fusion | flops 8598323200 | bytes 23068672 | tf_op jit(solution)/shard_map/dot_general | solution.py:156
  832.4 276.9 %reduce-scatter.2.cloned.1.call-done = bf16[512,4096]{1,0:T(8,128)(2,1)} async-done(((bf16[2048,4096]{1,0:T(8,128)(2,1)}), bf16[512,4096]{1,0:T(8,128)(2,1)}) %reduce-scatter.2.cloned.1.call-update) | async-done | bytes 4194320 | tf_op jit(solution)/shard_map/reduce_scatter | solution.py:155
  (209 shorter events, 376.7 us)
Async XLA Ops:
  6.5 7.0 copy-start.5
  6.5 13.3 %copy-start.13 = (s32[2]{0:T(128)S(1)}, s32[2]{0:T(128)}, u32[]{:S(2)}) copy-start(s32[2]{0:T(128)} %param.16) | copy-start | bytes 28
  6.5 1102.7 %reduce-scatter.2.cloned.1.call-start = ((), (), s32[]{:S(2)}) async-start(), calls=%async_computation.1 | async-start | bytes 20971520 | tf_op jit(solution)/shard_map/reduce_scatter | solution.py:155
  9.9 14.3 %collective-permute-start.3 = (bf16[2048,4,128]{2,0,1:T(8,128)(2,1)}, bf16[2048,4,128]{2,0,1:T(8,128)(2,1)}, u32[]{:S(2)}, u32[]{:S(2)}) collective-permute-start(bf16[2048,4,128]{2,0,1:T(8,128)(2,1)} %copy.21), channel_id=1, source_target_pairs={{0,4},{4,8},{8,12},{12,16},{16,20},{20,24},{24,28},{1,5},{5,9},{9,... | collective-permute-start | bytes 6291464 | tf_op jit(solution)/shard_map/ppermute | solution.py:19
  15.2 32.5 %collective-permute-start = (bf16[2048,4,128]{2,0,1:T(8,128)(2,1)}, bf16[2048,4,128]{2,0,1:T(8,128)(2,1)}, u32[]{:S(2)}, u32[]{:S(2)}) collective-permute-start(bf16[2048,4,128]{2,0,1:T(8,128)(2,1)} %copy.20), channel_id=1, source_target_pairs={{0,4},{4,8},{8,12},{12,16},{16,20},{20,24},{24,28},{1,5},{5,9},{9,... | collective-permute-start | bytes 6291464 | tf_op jit(solution)/shard_map/ppermute | solution.py:19
  24.2 23.5 %copy-start.6 = (bf16[2048,4,128]{2,1,0:T(4,128)(2,1)S(1)}, bf16[2048,4,128]{2,1,0:T(4,128)(2,1)}, u32[]{:S(2)}) copy-start(bf16[2048,4,128]{2,1,0:T(4,128)(2,1)} %param.13) | copy-start | bytes 6291460
  28.3 68.7 %collective-permute-start.4 = (bf16[2048,4,128]{2,0,1:T(8,128)(2,1)S(1)}, bf16[2048,4,128]{2,0,1:T(8,128)(2,1)}, u32[]{:S(2)}, u32[]{:S(2)}) collective-permute-start(bf16[2048,4,128]{2,0,1:T(8,128)(2,1)S(1)} %get-tuple-element.616), channel_id=1, source_target_pairs={{0,8},{4,12},{8,16},{12,20},{16,24},{20,28},{1,9},{5,13},{9,17},{1... | collective-permute-start | bytes 6291464 | tf_op jit(solution)/shard_map/ppermute | solution.py:19
  51.8 85.7 %collective-permute-start.1 = (bf16[2048,4,128]{2,0,1:T(8,128)(2,1)}, bf16[2048,4,128]{2,0,1:T(8,128)(2,1)}, u32[]{:S(2)}, u32[]{:S(2)}) collective-permute-start(bf16[2048,4,128]{2,0,1:T(8,128)(2,1)} %get-tuple-element.618), channel_id=1, source_target_pairs={{0,8},{4,12},{8,16},{12,20},{16,24},{20,28},{1,9},{5,13},{9,17},{1... | collective-permute-start | bytes 6291464 | tf_op jit(solution)/shard_map/ppermute | solution.py:19
  90.0 299.3 %collective-permute-start.8 = (bf16[2048,4,128]{2,0,1:T(8,128)(2,1)}, bf16[2048,4,128]{2,0,1:T(8,128)(2,1)}, u32[]{:S(2)}, u32[]{:S(2)}) collective-permute-start(bf16[2048,4,128]{2,0,1:T(8,128)(2,1)} %get-tuple-element.617), channel_id=1, source_target_pairs={{0,8},{4,12},{8,16},{12,20},{16,24},{20,28},{1,9},{5,13},{9,17},{1... | collective-permute-start | bytes 6291464 | tf_op jit(solution)/shard_map/ppermute | solution.py:19
  93.5 301.6 %collective-permute-start.6 = (bf16[2048,4,128]{2,0,1:T(8,128)(2,1)}, bf16[2048,4,128]{2,0,1:T(8,128)(2,1)}, u32[]{:S(2)}, u32[]{:S(2)}) collective-permute-start(bf16[2048,4,128]{2,0,1:T(8,128)(2,1)} %get-tuple-element.619), channel_id=1, source_target_pairs={{0,8},{4,12},{8,16},{12,20},{16,24},{20,28},{1,9},{5,13},{9,17},{1... | collective-permute-start | bytes 6291464 | tf_op jit(solution)/shard_map/ppermute | solution.py:19
  100.1 300.9 %collective-permute-start.5 = (bf16[2048,4,128]{2,0,1:T(8,128)(2,1)}, bf16[2048,4,128]{2,0,1:T(8,128)(2,1)}, u32[]{:S(2)}, u32[]{:S(2)}) collective-permute-start(bf16[2048,4,128]{2,0,1:T(8,128)(2,1)} %broadcast_select_fusion.10), channel_id=1, source_target_pairs={{0,16},{4,20},{8,24},{12,28},{1,17},{5,21},{9,25},{13,29},{2,18},{... | collective-permute-start | bytes 6291464 | tf_op jit(solution)/shard_map/ppermute | solution.py:19
  140.6 263.6 %collective-permute-start.2 = (bf16[2048,4,128]{2,0,1:T(8,128)(2,1)}, bf16[2048,4,128]{2,0,1:T(8,128)(2,1)}, u32[]{:S(2)}, u32[]{:S(2)}) collective-permute-start(bf16[2048,4,128]{2,0,1:T(8,128)(2,1)} %broadcast_select_fusion.11), channel_id=1, source_target_pairs={{0,16},{4,20},{8,24},{12,28},{1,17},{5,21},{9,25},{13,29},{2,18},{... | collective-permute-start | bytes 6291464 | tf_op jit(solution)/shard_map/ppermute | solution.py:19
  184.7 8.2 copy-start.3
  184.7 8.2 copy-start.2
  243.9 8.2 copy-start.3
  243.9 8.2 copy-start.2
  303.1 8.2 copy-start.3
  303.1 8.2 copy-start.2
  362.4 8.2 copy-start.3
  362.4 8.2 copy-start.2
  392.5 214.3 %collective-permute-start.9 = (bf16[2048,4,128]{2,0,1:T(8,128)(2,1)}, bf16[2048,4,128]{2,0,1:T(8,128)(2,1)}, u32[]{:S(2)}, u32[]{:S(2)}) collective-permute-start(bf16[2048,4,128]{2,0,1:T(8,128)(2,1)} %broadcast_select_fusion.4), channel_id=1, source_target_pairs={{0,16},{4,20},{8,24},{12,28},{1,17},{5,21},{9,25},{13,29},{2,18},{... | collective-permute-start | bytes 6291464 | tf_op jit(solution)/shard_map/ppermute | solution.py:19
  398.2 211.8 %collective-permute-start.7 = (bf16[2048,4,128]{2,0,1:T(8,128)(2,1)}, bf16[2048,4,128]{2,0,1:T(8,128)(2,1)}, u32[]{:S(2)}, u32[]{:S(2)}) collective-permute-start(bf16[2048,4,128]{2,0,1:T(8,128)(2,1)} %broadcast_select_fusion.5), channel_id=1, source_target_pairs={{0,16},{4,20},{8,24},{12,28},{1,17},{5,21},{9,25},{13,29},{2,18},{... | collective-permute-start | bytes 6291464 | tf_op jit(solution)/shard_map/ppermute | solution.py:19
  440.0 6.9 copy-start
  489.3 6.9 copy-start
  538.5 6.9 copy-start
  587.7 6.9 copy-start
  615.6 197.2 %copy-start.10 = (f32[4,512,4]{1,2,0:T(4,128)S(1)}, f32[4,512,4]{1,2,0:T(4,128)}, u32[]{:S(2)}) copy-start(f32[4,512,4]{1,2,0:T(4,128)} %copy-done.9) | copy-start | bytes 98308
  615.6 197.2 %copy-start.12 = (f32[4,512,4]{1,2,0:T(4,128)S(1)}, f32[4,512,4]{1,2,0:T(4,128)}, u32[]{:S(2)}) copy-start(f32[4,512,4]{1,2,0:T(4,128)} %copy-done.11) | copy-start | bytes 98308
  646.1 6.9 copy-start.1
  695.4 6.9 copy-start.1
  744.6 7.0 copy-start.1
  793.8 7.0 copy-start.1
  (6 other events, 22.3 us)
Sparse Core Ops, SparseCore 0:
  832.5 276.7 reduce-scatter.1
where the time goes:
time: 1120 us
  local copies, waits for them, and re-layouts  371 us (33%)
  waiting for transfers between devices  312 us (28%)
  matrix products  191 us (17%)
  other arithmetic  133 us (12%)
  starting transfers between devices  81.1 us (7%)
  between operations  20.4 us (2%)
    reduce_scatter x1, waiting for transfers between devices, per_device(): lax.psum_scatter(jnp.dot(flattened, weight_rows, preferred_element_type=j...  277 us
    broadcast_in_dim x12, local copies, waits for them, and re-layouts, one_block(): jnp.repeat(jnp.repeat(pattern_part > 0, BLOCK, axis=1), BLOCK, axis=2)  193 us
    reshape x12, local copies, waits for them, and re-layouts, one_block(): jnp.repeat(jnp.repeat(pattern_part > 0, BLOCK, axis=1), BLOCK, axis=2)  144 us
    dot_general x12, matrix products, one_block(): jnp.einsum('hqk,khe->qhe', weights.astype(jnp.bfloat16), value_part, pref...  91.8 us
    dot_general x12, matrix products, one_block(): jnp.einsum('qhe,khe->hqk', query_rows, key_part, preferred_element_type=j...  88.1 us
    ppermute x10, starting transfers between devices, from_behind(): lax.ppermute(value, axis, [(source, source + steps) for source in range(f...  81.1 us
    reduce_sum x12, other arithmetic, one_block(): row_total = jnp.sum(weights, axis=2)  74.5 us
    ppermute x10, waiting for transfers between devices, from_behind(): lax.ppermute(value, axis, [(source, source + steps) for source in range(f...  34.7 us
  transfers between devices with their start and end apart: 11, of which 2 were waited for; matrix products, arithmetic and copies ran while one was open for 42% of the time, Pallas kernels for 0%

commit v1 on v0

v1 whole, which is shorter than its diff:
```python
import functools

import jax
import jax.numpy as jnp
from jax import lax
from jax.experimental import pallas as pl
from jax.experimental.pallas import tpu as pltpu
from jax.sharding import PartitionSpec as P

BLOCK = 128
LANES = 128
STAT_ROWS = 16
NEG_FILL = -1e30
LEAST_PEAK = -5e29
LOG2E = 1.4426950408889634
NT = (((1,), (1,)), ((), ()))
VMEM_BYTES = 60 * 2**20


def kernel_call(body, name, micros, **options):
    return pl.pallas_call(
        body,
        name=name,
        cost_estimate=pl.CostEstimate(flops=int(micros * 1.15e9), bytes_accessed=1, transcendentals=0),
        compiler_params=pltpu.CompilerParams(vmem_limit_bytes=VMEM_BYTES),
        **options,
    )


def helper_job(info_ref, number):
    me, distance = info_ref[0], info_ref[2 + number]
    odd = distance & 1
    hops = (distance + odd * (1 - 2 * (me & 1))) >> 1
    query_shard = me + 2 * hops
    return hops, query_shard, query_shard - distance, odd


def bias_rows(pattern_ref, query_shard, key_shard, blocks, is_local):
    count = pattern_ref.shape[1] // blocks
    query_shard = jnp.clip(query_shard, 0, count - 1)
    key_shard = jnp.clip(key_shard, 0, count - 1)
    rows = pattern_ref[0, pl.ds(pl.multiple_of(query_shard * blocks, blocks), blocks), :]
    width = rows.shape[1]
    rows = pltpu.roll(rows, width - key_shard * blocks, 1)
    if width >= LANES:
        rows = rows[:, :LANES]
    else:
        rows = jnp.concatenate([rows, jnp.zeros((blocks, LANES - width), rows.dtype)], 1)
    query_block = lax.broadcasted_iota(jnp.int32, rows.shape, 0)
    key_block = lax.broadcasted_iota(jnp.int32, rows.shape, 1)
    seen = rows > 0
    if is_local:
        seen = seen & (key_block < query_block) | (key_block == query_block)
    return jnp.where(seen | (key_block >= blocks), 0.0, NEG_FILL)


def mark_blocks(ref):
    block_of = lax.broadcasted_iota(jnp.int32, ref.shape, 0) // BLOCK
    lane = lax.broadcasted_iota(jnp.int32, ref.shape, 1)
    ref[...] = jnp.where(block_of == lane, 1.0, 0.0).astype(jnp.bfloat16)


def prepare_body(info_ref, value_ref, pattern_ref, turned_value_ref, local_ref, *bias_refs, spots):
    tokens = value_ref.shape[0]
    turned_value_ref[0, :LANES, :] = value_ref[...].T
    turned_value_ref[0, LANES:, :] = jnp.ones((STAT_ROWS, tokens), jnp.bfloat16)
    local_ref[0] = bias_rows(pattern_ref, info_ref[0], info_ref[0], len(spots), True)
    for number, out_ref in enumerate(bias_refs):
        _, query_shard, key_shard, _ = helper_job(info_ref, number)
        rows = bias_rows(pattern_ref, query_shard, key_shard, len(spots), False)
        for block, spot in enumerate(spots):
            out_ref[0, spot : spot + 1, :] = rows[block : block + 1, :]


def prepare(info, values, block_pattern, spots):
    tokens, width = values.shape
    heads = width // LANES
    out_shapes = [(LANES + STAT_ROWS, tokens)] + [(len(spots), LANES)] * 3
    out_types = [jnp.bfloat16] + [jnp.float32] * 3
    return kernel_call(
        functools.partial(prepare_body, spots=spots),
        "prepare",
        4,
        grid=(heads,),
        in_specs=[
            pl.BlockSpec(memory_space=pltpu.SMEM),
            pl.BlockSpec((tokens, LANES), lambda h: (0, h)),
            pl.BlockSpec((1, *block_pattern.shape[1:]), lambda h: (h, 0, 0)),
        ],
        out_specs=[pl.BlockSpec((1, *shape), lambda h: (h, 0, 0)) for shape in out_shapes],
        out_shape=[
            jax.ShapeDtypeStruct((heads, *shape), kind) for shape, kind in zip(out_shapes, out_types)
        ],
    )(info, values, block_pattern)


def widen_queries(queries, bias_rows):
    scaled = (queries.astype(jnp.float32) * (LANES**-0.5 * LOG2E)).astype(jnp.bfloat16)
    rows = queries.shape[0] // len(bias_rows)
    bias = [jnp.broadcast_to(row, (rows, LANES)).astype(jnp.bfloat16) for row in bias_rows]
    return jnp.concatenate([scaled, jnp.concatenate(bias, 0)], 1)


def split_three(value):
    high = value.astype(jnp.bfloat16).astype(jnp.float32)
    rest = value - high
    middle = rest.astype(jnp.bfloat16).astype(jnp.float32)
    low = rest - middle
    return jnp.concatenate([high, middle, low, jnp.zeros_like(low)], 0)


def peak_eight(scores):
    return jnp.max(scores.reshape(scores.shape[0] // 8, 8, scores.shape[1]), 0)


def finish_rows(numerator, peak):
    total = jnp.maximum(numerator[LANES : LANES + 1], 1e-30)
    normal = (numerator[:LANES] * (1.0 / total)).astype(jnp.bfloat16)
    return normal, split_three(peak + jnp.log2(total))


def far_body(info_ref, *refs, places, tile, step, first_block):
    sources = 2
    query_refs, refs = refs[:places], refs[places:]
    key_refs, value_refs, bias_refs, out_refs, joined_ref, refs = (
        refs[:2],
        refs[2:4],
        refs[4:6],
        refs[6:8],
        refs[8],
        refs[9:],
    )
    (
        held_queries,
        held_bias,
        held_keys,
        held_values,
        marks,
        held_out,
        score_a,
        score_b,
        query_sems,
        key_sems,
        value_sems,
        out_sems,
    ) = refs
    heads, _, tokens = value_refs[0].shape
    jobs = [helper_job(info_ref, number) for number in range(sources)]
    rows = query_refs[0].shape[0]
    tiles = sources * rows // tile
    per_tile = tile // BLOCK
    per_source = rows // tile
    scores = (score_a, score_b)

    def query_copy(source, place):
        target = held_queries.at[source * rows : (source + 1) * rows, :]
        return pltpu.make_async_copy(query_refs[place], target, query_sems.at[source])

    def key_copy(source, head, owner):
        lanes = pl.ds(pl.multiple_of(head * LANES, LANES), LANES)
        return pltpu.make_async_copy(
            key_refs[owner].at[:, lanes], held_keys.at[source, head], key_sems.at[source, head]
        )

    def value_copy(source, head, owner):
        return pltpu.make_async_copy(
            value_refs[owner].at[head], held_values.at[source, head], value_sems.at[source, head]
        )

    for head in range(heads):
        for source, (hops, _, _, odd) in enumerate(jobs):
            if head == 0:
                for place in range(places):
                    pl.when(hops == place)(query_copy(source, place).start)
            for owner in range(2):

                @pl.when(odd == owner)
                def _(head=head, source=source, owner=owner):
                    key_copy(source, head, owner).start()
                    value_copy(source, head, owner).start()

    mark_blocks(marks)
    for source in range(sources):
        count = rows // BLOCK
        held_bias[:, source * count : (source + 1) * count, :] = bias_refs[source][
            :, first_block : first_block + count, :
        ]

    def load_queries(place, head):
        lanes = pl.ds(pl.multiple_of(head * LANES, LANES), LANES)
        block = held_queries[pl.ds(pl.multiple_of(place * tile, tile), tile), lanes]
        bias = [held_bias[head, pl.ds(place * per_tile + j, 1), :] for j in range(per_tile)]
        return widen_queries(block, bias)

    def score_step(queries, source, head, first, target):
        spot = slice(first, first + step)
        keys = jnp.concatenate([held_keys[source, head, spot, :], marks[spot, :]], 1)
        part = lax.dot_general(keys, queries, NT, preferred_element_type=jnp.float32)
        target[spot, :] = part
        return peak_eight(part)

    starts = range(0, tokens, step)

    def one_item(head, place, next_head, next_place, current, upcoming, peaks):
        source, next_source = place // per_source, next_place // per_source
        queries = load_queries(next_place, next_head)
        peak = jnp.maximum(jnp.max(peaks, 0, keepdims=True), LEAST_PEAK)
        peaks = numerator = None
        for first in starts:
            found = score_step(queries, next_source, next_head, first, upcoming)
            peaks = found if peaks is None else jnp.maximum(peaks, found)
            weights = jnp.exp2(current[first : first + step, :] - peak).astype(jnp.bfloat16)
            part = jnp.dot(
                held_values[source, head, :, first : first + step], weights, preferred_element_type=jnp.float32
            )
            numerator = part if numerator is None else numerator + part
        normal, three = finish_rows(numerator, peak)
        columns = pl.ds(pl.multiple_of(place * tile, tile), tile)
        held_out[head, :LANES, columns] = normal
        three = jnp.concatenate([three] * (STAT_ROWS // 4), 0).astype(jnp.bfloat16)
        held_out[head, LANES:, columns] = three
        return peaks

    pairs = tiles // 2

    def one_pair(number, peaks):
        head, place = number // pairs, number % pairs * 2
        peaks = one_item(head, place, head, place + 1, score_a, score_b, peaks)
        is_last = place + 2 == tiles
        next_head = jnp.where(is_last, jnp.minimum(head + 1, heads - 1), head)
        next_place = jnp.where(is_last, 0, place + 2)

        @pl.when(next_head != head)
        def _():
            for source in range(sources):
                key_copy(source, next_head, 0).wait()
                value_copy(source, next_head, 0).wait()

        return one_item(head, place + 1, next_head, next_place, score_b, score_a, peaks)

    query_copy(0, 0).wait()
    key_copy(0, 0, 0).wait()
    queries = load_queries(0, 0)
    peaks = None
    for first in starts:
        found = score_step(queries, 0, 0, first, score_a)
        peaks = found if peaks is None else jnp.maximum(peaks, found)
    query_copy(1, 0).wait()
    key_copy(1, 0, 0).wait()
    for source in range(sources):
        value_copy(source, 0, 0).wait()
    lax.fori_loop(0, heads * pairs, one_pair, peaks)
    copies = []
    last = places - 1

    def send_out(first, count, columns, target, number):
        copies.append(
            pltpu.make_async_copy(
                held_out.at[first, :count, columns],
                target.at[first * LANES : first * LANES + count, :],
                out_sems.at[number, first],
            )
        )
        copies[-1].start()

    both = [slice(source * rows, (source + 1) * rows) for source in range(sources)]
    for source, columns in enumerate(both):
        stats = [held_out[head, LANES : LANES + 4, columns] for head in range(heads)]
        if 4 * heads < STAT_ROWS:
            stats.append(jnp.zeros((STAT_ROWS - 4 * heads, rows), jnp.bfloat16))
        held_out[heads, :STAT_ROWS, columns] = jnp.concatenate(stats, 0)
        for head in range(heads + 1):
            send_out(head, LANES if head < heads else STAT_ROWS, columns, out_refs[source], source)
    joined = slice(sources * rows, (sources + 1) * rows)
    stats = []
    for head in range(heads):
        pieces = []
        for (hops, _, _, _), columns in zip(jobs, both):
            three = held_out[head, LANES : LANES + 3, columns].astype(jnp.float32)
            stat = jnp.sum(three, 0, keepdims=True)
            pieces.append((held_out[head, :LANES, columns], jnp.where(hops == last, stat, NEG_FILL)))
        held_out[head, :LANES, joined], stat = merge_many(pieces)
        stats.append(split_three(stat))
        send_out(head, LANES, joined, joined_ref, sources)
    if 4 * heads < STAT_ROWS:
        stats.append(jnp.zeros((STAT_ROWS - 4 * heads, rows), jnp.float32))
    held_out[heads, :STAT_ROWS, joined] = jnp.concatenate(stats, 0).astype(jnp.bfloat16)
    send_out(heads, STAT_ROWS, joined, joined_ref, sources)
    for copy in copies:
        copy.wait()


def attend_far(info, queries, keys, turned_values, biases, first_block):
    sources = 2
    heads, deep, tokens = turned_values[0].shape
    rows, width = queries[0].shape
    tile = min(256, rows)
    assert rows // tile * sources % 2 == 0 and rows % tile == 0
    anywhere, in_vmem = pl.BlockSpec(memory_space=pl.ANY), pl.BlockSpec(memory_space=pltpu.VMEM)
    return kernel_call(
        functools.partial(
            far_body, places=len(queries), tile=tile, step=min(512, tokens), first_block=first_block
        ),
        "attend_far",
        16,
        in_specs=[pl.BlockSpec(memory_space=pltpu.SMEM)]
        + [anywhere] * (len(queries) + 2 * sources)
        + [in_vmem] * sources,
        out_specs=[anywhere] * (sources + 1),
        out_shape=[jax.ShapeDtypeStruct((heads * LANES + STAT_ROWS, rows), jnp.bfloat16)] * (sources + 1),
        scratch_shapes=[
            pltpu.VMEM((sources * rows, width), jnp.bfloat16),
            pltpu.VMEM((heads, sources * rows // BLOCK, LANES), jnp.float32),
            pltpu.VMEM((sources, heads, tokens, LANES), jnp.bfloat16),
            pltpu.VMEM((sources, heads, deep, tokens), jnp.bfloat16),
            pltpu.VMEM((tokens, LANES), jnp.bfloat16),
            pltpu.VMEM((heads + 1, LANES + STAT_ROWS, (sources + 1) * rows), jnp.bfloat16),
            pltpu.VMEM((tokens, tile), jnp.float32),
            pltpu.VMEM((tokens, tile), jnp.float32),
            pltpu.SemaphoreType.DMA((sources,)),
            pltpu.SemaphoreType.DMA((sources, heads)),
            pltpu.SemaphoreType.DMA((sources, heads)),
            pltpu.SemaphoreType.DMA((sources + 1, heads + 1)),
        ],
    )(info, *queries, *keys, *turned_values, *biases)


def local_body(query_ref, key_ref, value_ref, bias_ref, out_ref, stat_ref, marks, score_a, score_b, *, tile, spots):
    tokens = key_ref.shape[0]
    tiles = tokens // tile
    per_tile = tile // BLOCK
    scores = (score_a, score_b)
    key_place = lax.broadcasted_iota(jnp.int32, (tile, tile), 0)
    query_place = lax.broadcasted_iota(jnp.int32, (tile, tile), 1)
    mark_blocks(marks)
    hidden = (key_place // BLOCK == query_place // BLOCK) & (key_place > query_place)

    def load_queries(place):
        rows = [bias_ref[0, place * per_tile + j : place * per_tile + j + 1, :] for j in range(per_tile)]
        return widen_queries(query_ref[place * tile : (place + 1) * tile, :], rows)

    def score_step(queries, place, number, target):
        spot = slice(number * tile, (number + 1) * tile)
        keys = jnp.concatenate([key_ref[spot, :], marks[spot, :]], 1)
        part = lax.dot_general(keys, queries, NT, preferred_element_type=jnp.float32)
        if number == place:
            part = jnp.where(hidden, NEG_FILL, part)
        target[number * tile : (number + 1) * tile, :] = part
        return peak_eight(part)

    peaks = score_step(load_queries(0), 0, 0, scores[0])
    for place in range(tiles):
        current, upcoming = scores[place % 2], scores[(place + 1) % 2]
        more = place + 1 < tiles
        queries = load_queries(place + 1) if more else None
        peak = jnp.max(peaks, 0, keepdims=True)
        peaks = numerator = None
        for number in range(place + 2):
            if more:
                found = score_step(queries, place + 1, number, upcoming)
                peaks = found if peaks is None else jnp.maximum(peaks, found)
            if number <= place:
                spot = slice(number * tile, (number + 1) * tile)
                weights = jnp.exp2(current[spot, :] - peak).astype(jnp.bfloat16)
                part = jnp.dot(value_ref[0, :, spot], weights, preferred_element_type=jnp.float32)
                numerator = part if numerator is None else numerator + part
        normal, stats = finish_rows(numerator, peak)
        stats = jnp.concatenate([stats] * (STAT_ROWS // 4), 0).astype(jnp.bfloat16)
        for j in range(per_tile):
            columns = pl.ds(spots[place * per_tile + j] * BLOCK, BLOCK)
            out_ref[:, columns] = normal[:, j * BLOCK : (j + 1) * BLOCK]
            stat_ref[0, :, columns] = stats[:, j * BLOCK : (j + 1) * BLOCK]


def attend_local(queries, keys, turned_values, bias, spots):
    tokens = keys.shape[0]
    tile = min(256, tokens)
    blocks = bias.shape[1]
    count = turned_values.shape[0]
    return kernel_call(
        functools.partial(local_body, tile=tile, spots=spots),
        "attend_local",
        18,
        grid=(count,),
        in_specs=[
            pl.BlockSpec((tokens, LANES), lambda h: (0, h)),
            pl.BlockSpec((tokens, LANES), lambda h: (0, h)),
            pl.BlockSpec((1, LANES + STAT_ROWS, tokens), lambda h: (h, 0, 0)),
            pl.BlockSpec((1, blocks, LANES), lambda h: (h, 0, 0)),
        ],
        out_specs=[
            pl.BlockSpec((LANES, tokens), lambda h: (h, 0)),
            pl.BlockSpec((1, STAT_ROWS, tokens), lambda h: (h, 0, 0)),
        ],
        out_shape=[
            jax.ShapeDtypeStruct((count * LANES, tokens), jnp.bfloat16),
            jax.ShapeDtypeStruct((count, STAT_ROWS, tokens), jnp.bfloat16),
        ],
        scratch_shapes=[pltpu.VMEM((tokens, LANES), jnp.bfloat16)]
        + [pltpu.VMEM((tokens, tile), jnp.float32)] * 2,
    )(queries, keys, turned_values, bias)


def packed_stats(ref, heads):
    first = heads * LANES
    return [
        sum(ref[p : p + 1, :].astype(jnp.float32) for p in range(first + 4 * head, first + 4 * head + 3))
        for head in range(heads)
    ]


def merge_many(pieces):
    peak = functools.reduce(jnp.maximum, [stat for _, stat in pieces])
    parts = [jnp.exp2(stat - peak) for _, stat in pieces]
    total = sum(parts)
    mixed = sum(piece.astype(jnp.float32) * (part / total) for (piece, _), part in zip(pieces, parts))
    return mixed.astype(jnp.bfloat16), peak + jnp.log2(total)


def merge_flags(info_ref, hops):
    own = [helper_job(info_ref, number)[0] == hops for number in range(2)]
    return [info_ref[0] >= 2, *own]


def merge_far_body(info_ref, *refs, heads, hops):
    piece_refs, out_ref = refs[:-1], refs[-1]
    flags = merge_flags(info_ref, hops)
    piece_stats = [packed_stats(ref, heads) for ref in piece_refs]
    stats = []
    for head in range(heads):
        rows = slice(head * LANES, (head + 1) * LANES)
        pieces = [
            (ref[rows, :], jnp.where(flag, stat[head], NEG_FILL))
            for ref, stat, flag in zip(piece_refs, piece_stats, flags)
        ]
        out_ref[rows, :], stat = merge_many(pieces)
        stats.append(split_three(stat))
    if 4 * heads < STAT_ROWS:
        stats.append(jnp.zeros((STAT_ROWS - 4 * heads, out_ref.shape[1]), jnp.float32))
    out_ref[heads * LANES :, :] = jnp.concatenate(stats, 0).astype(jnp.bfloat16)


def merge_far(info, pieces, heads, hops):
    in_vmem = pl.BlockSpec(memory_space=pltpu.VMEM)
    return kernel_call(
        functools.partial(merge_far_body, heads=heads, hops=hops),
        "merge_far",
        2.3,
        in_specs=[pl.BlockSpec(memory_space=pltpu.SMEM)] + [in_vmem] * len(pieces),
        out_specs=in_vmem,
        out_shape=jax.ShapeDtypeStruct(pieces[0].shape, jnp.bfloat16),
    )(info, *pieces)


def merge_local_body(info_ref, normal_ref, stat_ref, *refs, heads, stages):
    held_refs, out_ref = refs[:-1], refs[-1]
    others = len(held_refs) // stages
    groups, _, columns = out_ref.shape
    wide = columns // stages
    flags = merge_flags(info_ref, 0)
    slots = []
    for piece in range(groups):
        apart = info_ref[1] ^ piece
        slots.append(jnp.where(info_ref[0] & 1 == 1, bit_reverse(apart, groups.bit_length() - 1), apart))
    for stage in range(stages):
        lanes = slice(stage * groups * wide, (stage + 1) * groups * wide)
        here = held_refs[stage * others : (stage + 1) * others]
        far_stats = [packed_stats(ref, heads) for ref in here]
        for head in range(heads):
            rows = slice(head * LANES, (head + 1) * LANES)
            stat = sum(stat_ref[head, p : p + 1, lanes].astype(jnp.float32) for p in range(3))
            pieces = [(normal_ref[rows, lanes], stat)]
            pieces += [
                (ref[rows, :], jnp.where(flag, far_stat[head], NEG_FILL))
                for ref, far_stat, flag in zip(here, far_stats, flags)
            ]
            held, _ = merge_many(pieces)
            for piece in range(groups):
                out_ref[slots[piece], rows, stage * wide : (stage + 1) * wide] = held[
                    :, piece * wide : (piece + 1) * wide
                ]


def merge_local(info, local, first, stages, chunks, pieces, heads, groups):
    normal, stat = local
    columns = normal.shape[1] // chunks * stages
    assert first % stages == 0
    specs = [
        pl.BlockSpec(memory_space=pltpu.SMEM),
        pl.BlockSpec((normal.shape[0], columns), lambda i: (0, first // stages)),
        pl.BlockSpec((*stat.shape[:2], columns), lambda i: (0, 0, first // stages)),
    ]
    specs += [pl.BlockSpec(piece.shape, lambda i: (0, 0)) for piece in pieces]
    return kernel_call(
        functools.partial(merge_local_body, heads=heads, stages=stages),
        "merge_local",
        4,
        grid=(1,),
        in_specs=specs,
        out_specs=pl.BlockSpec((groups, heads * LANES, columns // groups), lambda i: (0, 0, 0)),
        out_shape=jax.ShapeDtypeStruct((groups, heads * LANES, columns // groups), jnp.bfloat16),
    )(info, normal, stat, *pieces)


def bit_reverse(place, bits):
    return sum((place >> bit & 1) << (bits - 1 - bit) for bit in range(bits))


def project_body(info_ref, weight_ref, *refs, sources, stages, cuts):
    bits = sources.bit_length() - 1
    own_refs, other_refs = refs[: sources - 1], refs[sources - 1 : 2 * sources - 2]
    part_refs = refs[2 * sources - 2 : 2 * sources - 2 + stages * sources]
    out_ref, held, sems = refs[-3:]
    depth, columns = weight_ref.shape
    half = depth // 2
    width = columns // cuts
    parity = info_ref[0] & 1
    copies = []
    for cut in range(cuts):
        lanes = slice(cut * width, (cut + 1) * width)
        pairs = [(weight_ref.at[:, lanes], held.at[cut, :depth, :])]
        for place in range(1, sources):
            own = pl.multiple_of(place * depth + parity * half, half)
            other = pl.multiple_of(bit_reverse(place, bits) * depth + (1 - parity) * half, half)
            pairs.append((own_refs[place - 1].at[:, lanes], held.at[cut, pl.ds(own, half), :]))
            pairs.append((other_refs[place - 1].at[:, lanes], held.at[cut, pl.ds(other, half), :]))
        copies.append(
            [
                pltpu.make_async_copy(origin, target, sems.at[cut, number])
                for number, (origin, target) in enumerate(pairs)
            ]
        )
        for copy in copies[-1]:
            copy.start()
    rows = [
        jnp.concatenate([part_refs[stage * sources + place][...].T for place in range(sources)], 1)
        for stage in range(stages)
    ]
    left = jnp.concatenate(rows, 0)
    for cut in range(cuts):
        for copy in copies[cut]:
            copy.wait()
        out_ref[:, cut * width : (cut + 1) * width] = jnp.dot(
            left, held[cut], preferred_element_type=jnp.float32
        ).astype(jnp.bfloat16)


def project(info, weight_rows, own, other, parts):
    sources, stages, cuts = len(parts[0]), len(parts), 4
    depth, columns = weight_rows.shape
    rows = sum(row[0].shape[1] for row in parts)
    anywhere, in_vmem = pl.BlockSpec(memory_space=pl.ANY), pl.BlockSpec(memory_space=pltpu.VMEM)
    flat = [piece for row in parts for piece in row]
    return kernel_call(
        functools.partial(project_body, sources=sources, stages=stages, cuts=cuts),
        "project",
        15,
        in_specs=[pl.BlockSpec(memory_space=pltpu.SMEM)]
        + [anywhere] * (2 * sources - 1)
        + [in_vmem] * len(flat),
        out_specs=in_vmem,
        out_shape=jax.ShapeDtypeStruct((rows, columns), jnp.bfloat16),
        scratch_shapes=[
            pltpu.VMEM((cuts, sources * depth, columns // cuts), jnp.bfloat16),
            pltpu.SemaphoreType.DMA((cuts, 2 * sources - 1)),
        ],
    )(info, weight_rows, *own, *other, *flat)


def shift(value, steps, first, last):
    return lax.ppermute(value, "ctx", [(source, source + steps) for source in range(first, last)])


def swap_sibling(value):
    return lax.ppermute(value, "ctx", [(i, i ^ 1) for i in range(lax.axis_size("ctx"))])


def swap_head(value, even_bits, odd_bits):
    count = lax.axis_size("head")
    pairs = []
    for place in range(lax.axis_size("ctx")):
        bits = odd_bits if place % 2 else even_bits
        pairs += [(place * count + i, place * count + (i ^ bits)) for i in range(count)]
    return lax.ppermute(value, ("ctx", "head"), pairs)


def gather_weights(weight_rows, parity, earlier):
    count = lax.axis_size("head")
    bits = count.bit_length() - 1
    half = weight_rows.shape[0] // 2
    weight_rows = after(weight_rows, earlier[0])
    held = [lax.dynamic_slice_in_dim(weight_rows, parity * half, half, 0)]
    for number in range(bits):
        sent = [after(piece, earlier[min(number, 1)]) for piece in held]
        held += [swap_head(piece, 1 << number, 1 << (bits - 1 - number)) for piece in sent]
    return held[1:], [swap_sibling(after(piece, earlier[2])) for piece in held[1:]]


def after(value, *earlier):
    return lax.optimization_barrier((value, *earlier))[0]


def chunk_of(array, axis, number, groups, chunks):
    shape = array.shape
    count = shape[axis] // (groups * chunks)
    split = array.reshape(shape[:axis] + (groups, chunks, count) + shape[axis + 1 :])
    piece = lax.index_in_dim(split, number, axis + 1, False)
    return piece.reshape(shape[:axis] + (groups * count,) + shape[axis + 1 :])


def per_device(query_states, key_states, value_states, block_pattern, helper_distances, out_weight):
    count = lax.axis_size("ctx")
    groups = lax.axis_size("head")
    me = lax.axis_index("ctx")
    group = lax.axis_index("head")
    tokens, heads, head_dim = query_states.shape
    blocks = tokens // BLOCK
    chunks = min(4, blocks // groups)
    per_piece = blocks // groups // chunks
    width = heads * head_dim
    parity = me & 1
    bits = groups.bit_length() - 1
    turns = [(place, bit_reverse(place, bits)) for place in range(groups)]
    weight_rows = out_weight.reshape(width, out_weight.shape[2])
    spots = []
    for block in range(blocks):
        part, rest = divmod(block, chunks * per_piece)
        spots.append((rest // per_piece * groups + part) * per_piece + rest % per_piece)

    def flat(array):
        return array.reshape(array.shape[0], width)

    def query_chunk(number):
        return flat(lax.optimization_barrier(chunk_of(query_states, 0, number, groups, chunks)))

    def exchange(pieces):
        return [pieces[0]] + [swap_head(pieces[place], *turns[place]) for place in range(1, groups)]

    places = count // 4
    info = jnp.concatenate([jnp.stack([me, group]), helper_distances])
    hops = [[query_chunk(number)] for number in range(chunks)]

    def move_down(number, *earlier):
        done = len(hops[number])
        moving = after(hops[number][-1], *earlier)
        hops[number].append(shift(moving, -2, 2, count - 2 * (done - 1)))

    for number in range(min(3, chunks)):
        move_down(number)
    keys = flat(key_states)
    turned_values, local_bias, *biases = prepare(info, flat(value_states), block_pattern, spots)
    both_keys = [keys, swap_sibling(keys)]
    both_values = [turned_values, swap_sibling(turned_values)]
    local = attend_local(flat(query_states), keys, turned_values, local_bias, spots)
    for number in range(3, chunks):
        move_down(number, hops[number - 3][1])
    for _ in range(1, places):
        for number in range(chunks):
            move_down(number)

    def attend(number, *earlier):
        arrays = [*hops[number][:-1], after(hops[number][-1], *earlier)]
        return attend_far(info, arrays, both_keys, both_values, biases, number * groups * per_piece)

    def move_up(piece, hops_left):
        return shift(piece, 2, 0, count - 2 * hops_left)

    def finish(first, stages, *earlier):
        pieces = [piece for number in range(first, first + stages) for piece in (moved[number], *own[number])]
        pieces[0] = after(pieces[0], *earlier)
        merged = merge_local(info, local, first, stages, chunks, pieces, heads, groups)
        return merged, exchange(merged)

    own, moved, parts = {}, {}, []
    last = local[0]
    weights = None
    for slot in range(chunks + places - 1):
        if slot < chunks:
            *own[slot], last = attend(slot, last)
            moved[slot] = move_up(last, places)
            if slot == min(1, chunks - 1):
                weights = gather_weights(weight_rows, parity, [local[0], own[0][0], last])
        for behind in range(1, places):
            number = slot - behind
            if 0 <= number < chunks:
                pieces = [after(moved[number], last), *own[number]]
                last = merge_far(info, pieces, heads, places - behind)
                moved[number] = move_up(last, places - behind)
    if chunks > 1:
        last, exchanged = finish(0, chunks - 1, last)
        parts.append(exchanged)
    last, exchanged = finish(chunks - 1, 1, last)
    parts.append(exchanged)
    return project(info, weight_rows, *weights, parts)


def solution(mesh):
    placed = (
        P("ctx", "head", None),
        P("ctx", "head", None),
        P("ctx", "head", None),
        P("head", None, None),
        P(),
        P("head", None, None),
    )
    return jax.shard_map(
        per_device, mesh=mesh, in_specs=placed, out_specs=P(("ctx", "head"), None), check_vma=False
    )
```

time: 1120 us -> 271 us (0.24)
  local copies, waits for them, and re-layouts: 371 us -> 17.6 us
  waiting for transfers between devices: 312 us -> 73.1 us
  matrix products: 191 us -> 0 us
  other arithmetic: 133 us -> 0.65 us
  Pallas kernels: 0 us -> 126 us
  starting transfers between devices: 81.1 us -> 52.3 us
  between operations: 20.4 us -> 0.59 us
    reduce_scatter x1 -> x0, waiting for transfers between devices: 277 us -> none  [per_device(): lax.psum_scatter(jnp.dot(flattened, weight_rows, preferred_element_type=j...]
    broadcast_in_dim x24 -> x0, local copies, waits for them, and re-layouts: 193 us -> none  [the longest x12 193 us: one_block(): jnp.repeat(jnp.repeat(pattern_part > 0, BLOCK, axis=1), BLOCK, axis=2)]
    dot_general x25 -> x0, matrix products: 191 us -> none  [the longest x12 91.8 us: one_block(): jnp.einsum('hqk,khe->qhe', weights.astype(jnp.bfloat16), value_part, pref...]
    reshape x12 -> x0, local copies, waits for them, and re-layouts: 144 us -> none  [one_block(): jnp.repeat(jnp.repeat(pattern_part > 0, BLOCK, axis=1), BLOCK, axis=2)]
    pallas_call x0 -> x13, Pallas kernels: none -> 126 us  [the longest x4 68.1 us: attend_far(): kernel_call(functools.partial(far_body, places=len(queries), tile=tile, s...]
    reduce_sum x12 -> x0, other arithmetic: 74.5 us -> none  [one_block(): row_total = jnp.sum(weights, axis=2)]
    ppermute x10 -> x30, waiting for transfers between devices: 34.7 us -> 73.1 us  [the longest x16 49.4 us: shift(): lax.ppermute(value, 'ctx', [(source, source + steps) for source in range(...]
    select_n x21 -> x0, other arithmetic: 34.2 us -> none  [the longest x10 33.5 us: pick_moved(): jnp.where(bit_on(hop_count, bit_number), after, before)]
  transfers between devices with their start and end apart: 11 -> 30, of which waited for: 2 -> 12; matrix products, arithmetic and copies ran while one was open for 42% -> 4% of each run, Pallas kernels for 0% -> 41%
where the time goes in v1:
time: 271 us; the launch traced here: 270 us
  Pallas kernels  126 us (46%)
  waiting for transfers between devices  73.1 us (27%)
  starting transfers between devices  52.3 us (19%)
  local copies, waits for them, and re-layouts  17.6 us (6%)
    pallas_call x4, Pallas kernels, attend_far(): kernel_call(functools.partial(far_body, places=len(queries), tile=tile, s...  68.1 us
    ppermute x16, waiting for transfers between devices, shift(): lax.ppermute(value, 'ctx', [(source, source + steps) for source in range(...  49.4 us
    ppermute x16, starting transfers between devices, shift(): lax.ppermute(value, 'ctx', [(source, source + steps) for source in range(...  39.5 us
    ppermute x9, waiting for transfers between devices, swap_head(): return lax.ppermute(value, ('ctx', 'head'), pairs)  23.7 us
    pallas_call x1, Pallas kernels, attend_local(): kernel_call(functools.partial(local_body, tile=tile, spots=spots), 'atten...  18.2 us
    pallas_call x1, Pallas kernels, project(): kernel_call(functools.partial(project_body, sources=sources, stages=stage...  15.3 us
    ppermute x9, starting transfers between devices, swap_head(): return lax.ppermute(value, ('ctx', 'head'), pairs)  11.7 us
    unnamed x49, local copies, waits for them, and re-layouts  10.8 us
  transfers between devices with their start and end apart: 30, of which 12 were waited for; matrix products, arithmetic and copies ran while one was open for 4% of the time, Pallas kernels for 41%

profile of v1, /device:TPU:0, one launch (start us, length us, event | category | flops | bytes accessed | tf_op | source)
XLA Modules:
  0.0 269.8 jit_solution(17673059390848647048)
XLA Ops:
  0.0 2.2 fusion
  9.0 4.4 %prepare.1 = (bf16[4,144,2048]{2,1,0:T(8,128)(2,1)}, f32[4,16,128]{2,1,0:T(8,128)}, f32[4,16,128]{2,1,0:T(8,128)}, f32[4,16,128]{2,1,0:T(8,128)}) custom-call(s32[4]{0:T(128)} %pad_add_fusion.info_ref, bf16[2048,512]{1,0:T(8,128)(2,1)} %bitcast.57, s32[4,128,128]{2,1,0:T(8,128)} %pattern_ref.1), custom_call_target="tpu_custom_call" | custom-call | flops 4600000000 | bytes 1 | tf_op jit(solution)/shard_map/prepare/pallas_call | solution.py:80
  18.8 2.3 collective-permute-done.1.refs_1_
  22.4 9.9 %collective-permute-done.7.refs_1_ = bf16[512,512]{1,0:T(8,128)(2,1)} collective-permute-done((bf16[512,512]{1,0:T(8,128)(2,1)}, bf16[512,512]{1,0:T(8,128)(2,1)}, u32[]{:S(2)}, u32[]{:S(2)}) %collective-permute-start.7) | collective-permute-done | bytes 524320 | tf_op jit(solution)/shard_map/ppermute | solution.py:571
  33.6 18.2 %attend_local.1 = (bf16[512,2048]{1,0:T(8,128)(2,1)}, bf16[4,16,2048]{2,1,0:T(8,128)(2,1)}) custom-call(bf16[2048,512]{1,0:T(8,128)(2,1)} %bitcast.56, bf16[2048,512]{1,0:T(8,128)(2,1)} %bitcast.46.key_ref.refs_3_, bf16[4,144,2048]{2,1,0:T(8,128)(2,1)} %get-tuple-element.41.value_ref.refs_5_, f32[4,16,128]{2,1,0:T(8,128)} %get-tuple-element.42.bias_ref), custom_call_target="tpu_custom_call" | custom-call | flops 20700000256 | bytes 1 | tf_op jit(solution)/shard_map/attend_local/pallas_call | solution.py:380
  53.7 2.0 collective-permute-start
  57.0 9.1 %collective-permute-done.14.refs_1_ = bf16[512,512]{1,0:T(8,128)(2,1)} collective-permute-done((bf16[512,512]{1,0:T(8,128)(2,1)S(1)}, bf16[512,512]{1,0:T(8,128)(2,1)}, u32[]{:S(2)}, u32[]{:S(2)}) %collective-permute-start.14) | collective-permute-done | bytes 524320 | tf_op jit(solution)/shard_map/ppermute | solution.py:571
  68.7 17.0 %attend_far.4 = (bf16[528,512]{1,0:T(8,128)(2,1)}, bf16[528,512]{1,0:T(8,128)(2,1)}, bf16[528,512]{1,0:T(8,128)(2,1)}) custom-call(s32[4]{0:T(128)} %pad_add_fusion.info_ref, bf16[512,512]{1,0:T(8,128)(2,1)} %bitcast.51.refs_0_, bf16[512,512]{1,0:T(8,128)(2,1)} %collective-permute-done.1.refs_1_, bf16[512,512]{1,0:T(8,128)(2,1)} %collective-permute-done.2.refs_2_, ...), custom_call_target="tpu_custom_call" | custom-call | flops 18400000000 | bytes 1 | tf_op jit(solution)/shard_map/attend_far/pallas_call | solution.py:300
  85.7 5.2 %collective-permute-start.12 = (bf16[528,512]{1,0:T(8,128)(2,1)}, bf16[528,512]{1,0:T(8,128)(2,1)S(1)}, u32[]{:S(2)}, u32[]{:S(2)}) collective-permute-start(bf16[528,512]{1,0:T(8,128)(2,1)} %get-tuple-element.52), channel_id=1, source_target_pairs={{0,8},{4,12},{8,16},{12,20},{1,9},{5,13},{9,17},{13,21},{2,10},{6,... | collective-permute-start | bytes 1622024 | tf_op jit(solution)/shard_map/ppermute | solution.py:571
  91.8 17.0 %attend_far.5 = (bf16[528,512]{1,0:T(8,128)(2,1)}, bf16[528,512]{1,0:T(8,128)(2,1)}, bf16[528,512]{1,0:T(8,128)(2,1)}) custom-call(s32[4]{0:T(128)} %pad_add_fusion.info_ref, bf16[512,512]{1,0:T(8,128)(2,1)} %bitcast.50.refs_0_, bf16[512,512]{1,0:T(8,128)(2,1)} %collective-permute-done.7.refs_1_, bf16[512,512]{1,0:T(8,128)(2,1)} %copy-done.14, ...), custom_call_target="tpu_custom_call" | custom-call | flops 18400000000 | bytes 1 | tf_op jit(solution)/shard_map/attend_far/pallas_call | solution.py:300
  108.8 5.1 %collective-permute-start.16 = (bf16[528,512]{1,0:T(8,128)(2,1)}, bf16[528,512]{1,0:T(8,128)(2,1)S(1)}, u32[]{:S(2)}, u32[]{:S(2)}) collective-permute-start(bf16[528,512]{1,0:T(8,128)(2,1)} %get-tuple-element.54), channel_id=1, source_target_pairs={{0,8},{4,12},{8,16},{12,20},{1,9},{5,13},{9,17},{13,21},{2,10},{6,... | collective-permute-start | bytes 1622024 | tf_op jit(solution)/shard_map/ppermute | solution.py:571
  116.6 2.6 merge_far.4
  119.2 17.0 %attend_far.6 = (bf16[528,512]{1,0:T(8,128)(2,1)}, bf16[528,512]{1,0:T(8,128)(2,1)}, bf16[528,512]{1,0:T(8,128)(2,1)}) custom-call(s32[4]{0:T(128)} %pad_add_fusion.info_ref, bf16[512,512]{1,0:T(8,128)(2,1)} %bitcast.67, bf16[512,512]{1,0:T(8,128)(2,1)} %copy-done.13, bf16[512,512]{1,0:T(8,128)(2,1)} %collective-permute-done.18.refs_2_, ...), custom_call_target="tpu_custom_call" | custom-call | flops 18400000000 | bytes 1 | tf_op jit(solution)/shard_map/attend_far/pallas_call | solution.py:300
  139.0 2.6 merge_far.5
  141.6 17.1 %attend_far.7 = (bf16[528,512]{1,0:T(8,128)(2,1)}, bf16[528,512]{1,0:T(8,128)(2,1)}, bf16[528,512]{1,0:T(8,128)(2,1)}) custom-call(s32[4]{0:T(128)} %pad_add_fusion.info_ref, bf16[512,512]{1,0:T(8,128)(2,1)} %bitcast.65, bf16[512,512]{1,0:T(8,128)(2,1)} %collective-permute-done.14.refs_1_, bf16[512,512]{1,0:T(8,128)(2,1)} %collective-permute-done.15.refs_2_, ...), custom_call_target="tpu_custom_call" | custom-call | flops 18400000000 | bytes 1 | tf_op jit(solution)/shard_map/attend_far/pallas_call | solution.py:300
  158.7 2.7 %collective-permute-start.19 = (bf16[528,512]{1,0:T(8,128)(2,1)}, bf16[528,512]{1,0:T(8,128)(2,1)}, u32[]{:S(2)}, u32[]{:S(2)}) collective-permute-start(bf16[528,512]{1,0:T(8,128)(2,1)} %get-tuple-element.68), channel_id=1, source_target_pairs={{0,8},{4,12},{8,16},{12,20},{1,9},{5,13},{9,17},{13,21},{2,10},{6,... | collective-permute-start | bytes 1622024 | tf_op jit(solution)/shard_map/ppermute | solution.py:571
  162.8 2.5 collective-permute-start.21
  165.3 2.6 merge_far.6
  167.9 5.7 %collective-permute-done.19.refs_0_ = bf16[528,512]{1,0:T(8,128)(2,1)} collective-permute-done((bf16[528,512]{1,0:T(8,128)(2,1)}, bf16[528,512]{1,0:T(8,128)(2,1)}, u32[]{:S(2)}, u32[]{:S(2)}) %collective-permute-start.19) | collective-permute-done | bytes 540704 | tf_op jit(solution)/shard_map/ppermute | solution.py:571
  173.6 5.2 %collective-permute-start.22 = (bf16[528,512]{1,0:T(8,128)(2,1)}, bf16[528,512]{1,0:T(8,128)(2,1)}, u32[]{:S(2)}, u32[]{:S(2)}) collective-permute-start(bf16[528,512]{1,0:T(8,128)(2,1)} %merge_far.6), channel_id=1, source_target_pairs={{0,8},{4,12},{8,16},{12,20},{16,24},{20,28},{1,9},{5,13},{9,17},{1... | collective-permute-start | bytes 1622024 | tf_op jit(solution)/shard_map/ppermute | solution.py:571
  178.8 2.6 merge_far.7
  181.4 3.7 %collective-permute-done.13.refs_0_ = bf16[528,512]{1,0:T(8,128)(2,1)S(1)} collective-permute-done((bf16[528,512]{1,0:T(8,128)(2,1)S(1)}, bf16[528,512]{1,0:T(8,128)(2,1)S(1)}, u32[]{:S(2)}, u32[]{:S(2)}) %collective-permute-start.13) | collective-permute-done | bytes 540704 | tf_op jit(solution)/shard_map/ppermute | solution.py:571
  185.1 5.2 %collective-permute-start.26 = (bf16[528,512]{1,0:T(8,128)(2,1)}, bf16[528,512]{1,0:T(8,128)(2,1)}, u32[]{:S(2)}, u32[]{:S(2)}) collective-permute-start(bf16[528,512]{1,0:T(8,128)(2,1)} %merge_far.7), channel_id=1, source_target_pairs={{0,8},{4,12},{8,16},{12,20},{16,24},{20,28},{1,9},{5,13},{9,17},{1... | collective-permute-start | bytes 1622024 | tf_op jit(solution)/shard_map/ppermute | solution.py:571
  190.8 6.0 %collective-permute-done.21.refs_3_ = bf16[528,512]{1,0:T(8,128)(2,1)} collective-permute-done((bf16[528,512]{1,0:T(8,128)(2,1)}, bf16[528,512]{1,0:T(8,128)(2,1)}, u32[]{:S(2)}, u32[]{:S(2)}) %collective-permute-start.21) | collective-permute-done | bytes 540704 | tf_op jit(solution)/shard_map/ppermute | solution.py:571
  196.8 11.6 %collective-permute-done.22.refs_6_ = bf16[528,512]{1,0:T(8,128)(2,1)} collective-permute-done((bf16[528,512]{1,0:T(8,128)(2,1)}, bf16[528,512]{1,0:T(8,128)(2,1)}, u32[]{:S(2)}, u32[]{:S(2)}) %collective-permute-start.22) | collective-permute-done | bytes 540704 | tf_op jit(solution)/shard_map/ppermute | solution.py:571
  208.4 6.0 %merge_local.2 = bf16[4,512,384]{2,1,0:T(8,128)(2,1)} custom-call(s32[4]{0:T(128)} %pad_add_fusion.info_ref, bf16[512,2048]{1,0:T(8,128)(2,1)} %get-tuple-element.43.normal_ref, bf16[4,16,2048]{2,1,0:T(8,128)(2,1)} %get-tuple-element.58.stat_ref, bf16[528,512]{1,0:T(8,128)(2,1)} %copy-done.9, bf16[528,512]{1,0:T(8,128)(2,1)} %get-tuple-element.49.refs_1_, ...), custom_call_target="tpu_custom_call" | custom-call | flops 4600000000 | bytes 1 | tf_op jit(solution)/shard_map/merge_local/pallas_call | solution.py:494
  215.6 3.1 %merge_local.3 = bf16[4,512,128]{2,1,0:T(8,128)(2,1)} custom-call(s32[4]{0:T(128)} %pad_add_fusion.info_ref, bf16[512,2048]{1,0:T(8,128)(2,1)} %get-tuple-element.43.normal_ref, bf16[4,16,2048]{2,1,0:T(8,128)(2,1)} %get-tuple-element.58.stat_ref, bf16[528,512]{1,0:T(8,128)(2,1)} %collective-permute-done.26.refs_0_, ...), custom_call_target="tpu_custom_call" | custom-call | flops 4600000000 | bytes 1 | tf_op jit(solution)/shard_map/merge_local/pallas_call | solution.py:494
  223.4 2.1 collective-permute-done.27.refs_11_
  227.3 4.0 %collective-permute-done.28.refs_12_ = bf16[512,128]{1,0:T(8,128)(2,1)S(1)} collective-permute-done((bf16[512,128]{1,0:T(8,128)(2,1)S(1)}, bf16[512,128]{1,0:T(8,128)(2,1)S(1)}, u32[]{:S(2)}, u32[]{:S(2)}) %collective-permute-start.28) | collective-permute-done | bytes 131104 | tf_op jit(solution)/shard_map/ppermute | solution.py:584
  232.8 5.8 %collective-permute-done.29.refs_13_ = bf16[512,128]{1,0:T(8,128)(2,1)S(1)} collective-permute-done((bf16[512,128]{1,0:T(8,128)(2,1)S(1)}, bf16[512,128]{1,0:T(8,128)(2,1)S(1)}, u32[]{:S(2)}, u32[]{:S(2)}) %collective-permute-start.29) | collective-permute-done | bytes 131104 | tf_op jit(solution)/shard_map/ppermute | solution.py:584
  240.8 11.9 %collective-permute-done.24.refs_8_ = bf16[512,384]{1,0:T(8,128)(2,1)S(1)} collective-permute-done((bf16[512,384]{1,0:T(8,128)(2,1)S(1)}, bf16[512,384]{1,0:T(8,128)(2,1)S(1)}, u32[]{:S(2)}, u32[]{:S(2)}) %collective-permute-start.24) | collective-permute-done | bytes 393248 | tf_op jit(solution)/shard_map/ppermute | solution.py:584
  254.3 15.3 %project.1 = bf16[512,4096]{1,0:T(8,128)(2,1)} custom-call(s32[4]{0:T(128)} %pad_add_fusion.info_ref, bf16[512,4096]{1,0:T(8,128)(2,1)} %bitcast.63, bf16[256,4096]{1,0:T(8,128)(2,1)} %collective-permute-done.refs_0_, bf16[256,4096]{1,0:T(8,128)(2,1)} %collective-permute-done.5.refs_1_, bf16[256,4096]{1,0:T(8,128)(2,1)} %collective-permute-done.6.refs_2_, ...), custom_call_target="tpu_custom_call" | custom-call | flops 17250000896 | bytes 1 | tf_op jit(solution)/shard_map/project/pallas_call | solution.py:554
  (95 shorter events, 41.5 us)
Async XLA Ops:
  3.1 18.0 %collective-permute-start.1 = (bf16[512,512]{1,0:T(8,128)(2,1)}, bf16[512,512]{1,0:T(8,128)(2,1)}, u32[]{:S(2)}, u32[]{:S(2)}) collective-permute-start(bf16[512,512]{1,0:T(8,128)(2,1)} %bitcast.51.refs_0_), channel_id=1, source_target_pairs={{8,0},{12,4},{16,8},{20,12},{24,16},{28,20},{9,1},{13,5},{17,9},{2... | collective-permute-start | bytes 1572872 | tf_op jit(solution)/shard_map/ppermute | solution.py:571
  5.3 27.0 %collective-permute-start.7 = (bf16[512,512]{1,0:T(8,128)(2,1)}, bf16[512,512]{1,0:T(8,128)(2,1)}, u32[]{:S(2)}, u32[]{:S(2)}) collective-permute-start(bf16[512,512]{1,0:T(8,128)(2,1)} %bitcast.50.refs_0_), channel_id=1, source_target_pairs={{8,0},{12,4},{16,8},{20,12},{24,16},{28,20},{9,1},{13,5},{17,9},{2... | collective-permute-start | bytes 1572872 | tf_op jit(solution)/shard_map/ppermute | solution.py:571
  13.4 55.3 %collective-permute-start.4 = (bf16[4,144,2048]{2,1,0:T(8,128)(2,1)}, bf16[4,144,2048]{2,1,0:T(8,128)(2,1)}, u32[]{:S(2)}, u32[]{:S(2)}) collective-permute-start(bf16[4,144,2048]{2,1,0:T(8,128)(2,1)} %get-tuple-element.41.value_ref.refs_5_), channel_id=1, source_target_pairs={{0,4},{4,0},{8,12},{12,8},{16,20},{20,16},{24,28},{28,24},{1,5},{5... | collective-permute-start | bytes 7077896 | tf_op jit(solution)/shard_map/ppermute | solution.py:575
  15.6 51.8 %collective-permute-start.3 = (bf16[2048,512]{1,0:T(8,128)(2,1)}, bf16[2048,512]{1,0:T(8,128)(2,1)}, u32[]{:S(2)}, u32[]{:S(2)}) collective-permute-start(bf16[2048,512]{1,0:T(8,128)(2,1)} %bitcast.46.key_ref.refs_3_), channel_id=1, source_target_pairs={{0,4},{4,0},{8,12},{12,8},{16,20},{20,16},{24,28},{28,24},{1,5},{5... | collective-permute-start | bytes 6291464 | tf_op jit(solution)/shard_map/ppermute | solution.py:575
  15.7 37.9 %collective-permute-start.17 = (bf16[512,512]{1,0:T(8,128)(2,1)S(1)}, bf16[512,512]{1,0:T(8,128)(2,1)S(1)}, u32[]{:S(2)}, u32[]{:S(2)}) collective-permute-start(bf16[512,512]{1,0:T(8,128)(2,1)S(1)} %bitcast.66), channel_id=1, source_target_pairs={{8,0},{12,4},{16,8},{20,12},{24,16},{28,20},{9,1},{13,5},{17,9},{2... | collective-permute-start | bytes 1572872 | tf_op jit(solution)/shard_map/ppermute | solution.py:571
  18.8 33.0 %copy-start.4 = (bf16[64,8,4,128]{3,1,2,0:T(8,128)(2,1)}, bf16[64,8,4,128]{3,1,2,0:T(8,128)(2,1)S(1)}, u32[]{:S(2)}) copy-start(bf16[64,8,4,128]{3,1,2,0:T(8,128)(2,1)S(1)} %copy.25) | copy-start | bytes 1572868
  21.1 34.6 %collective-permute-start.2 = (bf16[512,512]{1,0:T(8,128)(2,1)}, bf16[512,512]{1,0:T(8,128)(2,1)}, u32[]{:S(2)}, u32[]{:S(2)}) collective-permute-start(bf16[512,512]{1,0:T(8,128)(2,1)} %collective-permute-done.1.refs_1_), channel_id=1, source_target_pairs={{8,0},{12,4},{16,8},{20,12},{9,1},{13,5},{17,9},{21,13},{10,2},{14... | collective-permute-start | bytes 1572872 | tf_op jit(solution)/shard_map/ppermute | solution.py:571
  32.4 33.7 %collective-permute-start.14 = (bf16[512,512]{1,0:T(8,128)(2,1)S(1)}, bf16[512,512]{1,0:T(8,128)(2,1)}, u32[]{:S(2)}, u32[]{:S(2)}) collective-permute-start(bf16[512,512]{1,0:T(8,128)(2,1)S(1)} %bitcast.64), channel_id=1, source_target_pairs={{8,0},{12,4},{16,8},{20,12},{24,16},{28,20},{9,1},{13,5},{17,9},{2... | collective-permute-start | bytes 1572872 | tf_op jit(solution)/shard_map/ppermute | solution.py:571
  53.6 32.1 %copy-start.13 = (bf16[512,512]{1,0:T(8,128)(2,1)}, bf16[512,512]{1,0:T(8,128)(2,1)S(1)}, u32[]{:S(2)}) copy-start(bf16[512,512]{1,0:T(8,128)(2,1)S(1)} %collective-permute-done.17.refs_1_) | copy-start | bytes 1572868
  53.7 60.2 %collective-permute-start = (bf16[256,4096]{1,0:T(8,128)(2,1)S(1)}, bf16[256,4096]{1,0:T(8,128)(2,1)}, u32[]{:S(2)}, u32[]{:S(2)}) collective-permute-start(bf16[256,4096]{1,0:T(8,128)(2,1)S(1)} %constant_dynamic-slice_fusion), channel_id=1, source_target_pairs={{0,1},{1,0},{2,3},{3,2},{4,6},{5,7},{6,4},{7,5},{8,9},{9,8},{10,11... | collective-permute-start | bytes 6291464 | tf_op jit(solution)/shard_map/ppermute | solution.py:584
  55.7 35.3 %collective-permute-start.8 = (bf16[512,512]{1,0:T(8,128)(2,1)}, bf16[512,512]{1,0:T(8,128)(2,1)S(1)}, u32[]{:S(2)}, u32[]{:S(2)}) collective-permute-start(bf16[512,512]{1,0:T(8,128)(2,1)} %collective-permute-done.7.refs_1_), channel_id=1, source_target_pairs={{8,0},{12,4},{16,8},{20,12},{9,1},{13,5},{17,9},{21,13},{10,2},{14... | collective-permute-start | bytes 1572872 | tf_op jit(solution)/shard_map/ppermute | solution.py:571
  66.1 53.1 %collective-permute-start.18 = (bf16[512,512]{1,0:T(8,128)(2,1)S(1)}, bf16[512,512]{1,0:T(8,128)(2,1)}, u32[]{:S(2)}, u32[]{:S(2)}) collective-permute-start(bf16[512,512]{1,0:T(8,128)(2,1)S(1)} %collective-permute-done.17.refs_1_), channel_id=1, source_target_pairs={{8,0},{12,4},{16,8},{20,12},{9,1},{13,5},{17,9},{21,13},{10,2},{14... | collective-permute-start | bytes 1572872 | tf_op jit(solution)/shard_map/ppermute | solution.py:571
  67.4 74.3 %collective-permute-start.15 = (bf16[512,512]{1,0:T(8,128)(2,1)}, bf16[512,512]{1,0:T(8,128)(2,1)}, u32[]{:S(2)}, u32[]{:S(2)}) collective-permute-start(bf16[512,512]{1,0:T(8,128)(2,1)} %collective-permute-done.14.refs_1_), channel_id=1, source_target_pairs={{8,0},{12,4},{16,8},{20,12},{9,1},{13,5},{17,9},{21,13},{10,2},{14... | collective-permute-start | bytes 1572872 | tf_op jit(solution)/shard_map/ppermute | solution.py:571
  85.7 30.1 %collective-permute-start.12 = (bf16[528,512]{1,0:T(8,128)(2,1)}, bf16[528,512]{1,0:T(8,128)(2,1)S(1)}, u32[]{:S(2)}, u32[]{:S(2)}) collective-permute-start(bf16[528,512]{1,0:T(8,128)(2,1)} %get-tuple-element.52), channel_id=1, source_target_pairs={{0,8},{4,12},{8,16},{12,20},{1,9},{5,13},{9,17},{13,21},{2,10},{6,... | collective-permute-start | bytes 1622024 | tf_op jit(solution)/shard_map/ppermute | solution.py:571
  108.8 29.4 %collective-permute-start.16 = (bf16[528,512]{1,0:T(8,128)(2,1)}, bf16[528,512]{1,0:T(8,128)(2,1)S(1)}, u32[]{:S(2)}, u32[]{:S(2)}) collective-permute-start(bf16[528,512]{1,0:T(8,128)(2,1)} %get-tuple-element.54), channel_id=1, source_target_pairs={{0,8},{4,12},{8,16},{12,20},{1,9},{5,13},{9,17},{13,21},{2,10},{6,... | collective-permute-start | bytes 1622024 | tf_op jit(solution)/shard_map/ppermute | solution.py:571
  113.9 76.4 %collective-permute-start.6 = (bf16[256,4096]{1,0:T(8,128)(2,1)}, bf16[256,4096]{1,0:T(8,128)(2,1)}, u32[]{:S(2)}, u32[]{:S(2)}) collective-permute-start(bf16[256,4096]{1,0:T(8,128)(2,1)} %collective-permute-done.refs_0_), channel_id=1, source_target_pairs={{0,2},{1,3},{2,0},{3,1},{4,5},{5,4},{6,7},{7,6},{8,10},{9,11},{10,... | collective-permute-start | bytes 6291464 | tf_op jit(solution)/shard_map/ppermute | solution.py:584
  115.8 74.5 %collective-permute-start.5 = (bf16[256,4096]{1,0:T(8,128)(2,1)S(1)}, bf16[256,4096]{1,0:T(8,128)(2,1)}, u32[]{:S(2)}, u32[]{:S(2)}) collective-permute-start(bf16[256,4096]{1,0:T(8,128)(2,1)S(1)} %constant_dynamic-slice_fusion), channel_id=1, source_target_pairs={{0,2},{1,3},{2,0},{3,1},{4,5},{5,4},{6,7},{7,6},{8,10},{9,11},{10,... | collective-permute-start | bytes 6291464 | tf_op jit(solution)/shard_map/ppermute | solution.py:584
  136.2 26.5 %collective-permute-start.20 = (bf16[528,512]{1,0:T(8,128)(2,1)}, bf16[528,512]{1,0:T(8,128)(2,1)S(1)}, u32[]{:S(2)}, u32[]{:S(2)}) collective-permute-start(bf16[528,512]{1,0:T(8,128)(2,1)} %get-tuple-element.63), channel_id=1, source_target_pairs={{0,8},{4,12},{8,16},{12,20},{1,9},{5,13},{9,17},{13,21},{2,10},{6,... | collective-permute-start | bytes 1622024 | tf_op jit(solution)/shard_map/ppermute | solution.py:571
  158.7 14.9 %collective-permute-start.19 = (bf16[528,512]{1,0:T(8,128)(2,1)}, bf16[528,512]{1,0:T(8,128)(2,1)}, u32[]{:S(2)}, u32[]{:S(2)}) collective-permute-start(bf16[528,512]{1,0:T(8,128)(2,1)} %get-tuple-element.68), channel_id=1, source_target_pairs={{0,8},{4,12},{8,16},{12,20},{1,9},{5,13},{9,17},{13,21},{2,10},{6,... | collective-permute-start | bytes 1622024 | tf_op jit(solution)/shard_map/ppermute | solution.py:571
  161.4 23.7 %collective-permute-start.13 = (bf16[528,512]{1,0:T(8,128)(2,1)S(1)}, bf16[528,512]{1,0:T(8,128)(2,1)S(1)}, u32[]{:S(2)}, u32[]{:S(2)}) collective-permute-start(bf16[528,512]{1,0:T(8,128)(2,1)S(1)} %copy-done.8), channel_id=1, source_target_pairs={{0,8},{4,12},{8,16},{12,20},{16,24},{20,28},{1,9},{5,13},{9,17},{1... | collective-permute-start | bytes 1622024 | tf_op jit(solution)/shard_map/ppermute | solution.py:571
  162.8 34.0 %collective-permute-start.21 = (bf16[528,512]{1,0:T(8,128)(2,1)}, bf16[528,512]{1,0:T(8,128)(2,1)}, u32[]{:S(2)}, u32[]{:S(2)}) collective-permute-start(bf16[528,512]{1,0:T(8,128)(2,1)} %merge_far.5), channel_id=1, source_target_pairs={{0,8},{4,12},{8,16},{12,20},{16,24},{20,28},{1,9},{5,13},{9,17},{1... | collective-permute-start | bytes 1622024 | tf_op jit(solution)/shard_map/ppermute | solution.py:571
  173.6 34.8 %collective-permute-start.22 = (bf16[528,512]{1,0:T(8,128)(2,1)}, bf16[528,512]{1,0:T(8,128)(2,1)}, u32[]{:S(2)}, u32[]{:S(2)}) collective-permute-start(bf16[528,512]{1,0:T(8,128)(2,1)} %merge_far.6), channel_id=1, source_target_pairs={{0,8},{4,12},{8,16},{12,20},{16,24},{20,28},{1,9},{5,13},{9,17},{1... | collective-permute-start | bytes 1622024 | tf_op jit(solution)/shard_map/ppermute | solution.py:571
  185.1 30.5 %collective-permute-start.26 = (bf16[528,512]{1,0:T(8,128)(2,1)}, bf16[528,512]{1,0:T(8,128)(2,1)}, u32[]{:S(2)}, u32[]{:S(2)}) collective-permute-start(bf16[528,512]{1,0:T(8,128)(2,1)} %merge_far.7), channel_id=1, source_target_pairs={{0,8},{4,12},{8,16},{12,20},{16,24},{20,28},{1,9},{5,13},{9,17},{1... | collective-permute-start | bytes 1622024 | tf_op jit(solution)/shard_map/ppermute | solution.py:571
  190.3 62.5 %collective-permute-start.9 = (bf16[256,4096]{1,0:T(8,128)(2,1)}, bf16[256,4096]{1,0:T(8,128)(2,1)}, u32[]{:S(2)}, u32[]{:S(2)}) collective-permute-start(bf16[256,4096]{1,0:T(8,128)(2,1)} %collective-permute-done.refs_0_), channel_id=1, source_target_pairs={{0,4},{4,0},{8,12},{12,8},{16,20},{20,16},{24,28},{28,24},{1,5},{5... | collective-permute-start | bytes 6291464 | tf_op jit(solution)/shard_map/ppermute | solution.py:575
  190.3 62.5 %collective-permute-start.11 = (bf16[256,4096]{1,0:T(8,128)(2,1)}, bf16[256,4096]{1,0:T(8,128)(2,1)S(1)}, u32[]{:S(2)}, u32[]{:S(2)}) collective-permute-start(bf16[256,4096]{1,0:T(8,128)(2,1)} %collective-permute-done.6.refs_2_), channel_id=1, source_target_pairs={{0,4},{4,0},{8,12},{12,8},{16,20},{20,16},{24,28},{28,24},{1,5},{5... | collective-permute-start | bytes 6291464 | tf_op jit(solution)/shard_map/ppermute | solution.py:575
  196.8 56.0 %collective-permute-start.10 = (bf16[256,4096]{1,0:T(8,128)(2,1)}, bf16[256,4096]{1,0:T(8,128)(2,1)}, u32[]{:S(2)}, u32[]{:S(2)}) collective-permute-start(bf16[256,4096]{1,0:T(8,128)(2,1)} %collective-permute-done.5.refs_1_), channel_id=1, source_target_pairs={{0,4},{4,0},{8,12},{12,8},{16,20},{20,16},{24,28},{28,24},{1,5},{5... | collective-permute-start | bytes 6291464 | tf_op jit(solution)/shard_map/ppermute | solution.py:575
  220.5 5.0 %collective-permute-start.27 = (bf16[512,128]{1,0:T(8,128)(2,1)S(1)}, bf16[512,128]{1,0:T(8,128)(2,1)S(1)}, u32[]{:S(2)}, u32[]{:S(2)}) collective-permute-start(bf16[512,128]{1,0:T(8,128)(2,1)S(1)} %get-tuple-element.87), channel_id=1, source_target_pairs={{0,1},{1,0},{2,3},{3,2},{4,6},{5,7},{6,4},{7,5},{8,9},{9,8},{10,11... | collective-permute-start | bytes 393224 | tf_op jit(solution)/shard_map/ppermute | solution.py:584
  222.3 18.1 %collective-permute-start.23 = (bf16[512,384]{1,0:T(8,128)(2,1)S(1)}, bf16[512,384]{1,0:T(8,128)(2,1)S(1)}, u32[]{:S(2)}, u32[]{:S(2)}) collective-permute-start(bf16[512,384]{1,0:T(8,128)(2,1)S(1)} %get-tuple-element.83), channel_id=1, source_target_pairs={{0,1},{1,0},{2,3},{3,2},{4,6},{5,7},{6,4},{7,5},{8,9},{9,8},{10,11... | collective-permute-start | bytes 1179656 | tf_op jit(solution)/shard_map/ppermute | solution.py:584
  225.5 5.7 %collective-permute-start.28 = (bf16[512,128]{1,0:T(8,128)(2,1)S(1)}, bf16[512,128]{1,0:T(8,128)(2,1)S(1)}, u32[]{:S(2)}, u32[]{:S(2)}) collective-permute-start(bf16[512,128]{1,0:T(8,128)(2,1)S(1)} %get-tuple-element.86), channel_id=1, source_target_pairs={{0,2},{1,3},{2,0},{3,1},{4,5},{5,4},{6,7},{7,6},{8,10},{9,11},{10,... | collective-permute-start | bytes 393224 | tf_op jit(solution)/shard_map/ppermute | solution.py:584
  231.2 7.3 %collective-permute-start.29 = (bf16[512,128]{1,0:T(8,128)(2,1)S(1)}, bf16[512,128]{1,0:T(8,128)(2,1)S(1)}, u32[]{:S(2)}, u32[]{:S(2)}) collective-permute-start(bf16[512,128]{1,0:T(8,128)(2,1)S(1)} %get-tuple-element.85), channel_id=1, source_target_pairs={{0,3},{1,2},{2,1},{3,0},{4,7},{5,6},{6,5},{7,4},{8,11},{9,10},{10,... | collective-permute-start | bytes 393224 | tf_op jit(solution)/shard_map/ppermute | solution.py:584
  238.5 14.2 %collective-permute-start.24 = (bf16[512,384]{1,0:T(8,128)(2,1)S(1)}, bf16[512,384]{1,0:T(8,128)(2,1)S(1)}, u32[]{:S(2)}, u32[]{:S(2)}) collective-permute-start(bf16[512,384]{1,0:T(8,128)(2,1)S(1)} %get-tuple-element.82), channel_id=1, source_target_pairs={{0,2},{1,3},{2,0},{3,1},{4,5},{5,4},{6,7},{7,6},{8,10},{9,11},{10,... | collective-permute-start | bytes 1179656 | tf_op jit(solution)/shard_map/ppermute | solution.py:584
  240.5 12.3 %collective-permute-start.25 = (bf16[512,384]{1,0:T(8,128)(2,1)S(1)}, bf16[512,384]{1,0:T(8,128)(2,1)S(1)}, u32[]{:S(2)}, u32[]{:S(2)}) collective-permute-start(bf16[512,384]{1,0:T(8,128)(2,1)S(1)} %get-tuple-element.81), channel_id=1, source_target_pairs={{0,3},{1,2},{2,1},{3,0},{4,7},{5,6},{6,5},{7,4},{8,11},{9,10},{10,... | collective-permute-start | bytes 1179656 | tf_op jit(solution)/shard_map/ppermute | solution.py:584
  (19 other events, 131.6 us)

commit v2 on v1

--- a/solution.py
+++ b/solution.py
@@ -167,18 +167,19 @@
             value_refs[owner].at[head], held_values.at[source, head], value_sems.at[source, head]
         )
 
-    for head in range(heads):
-        for source, (hops, _, _, odd) in enumerate(jobs):
-            if head == 0:
-                for place in range(places):
-                    pl.when(hops == place)(query_copy(source, place).start)
+    def start_head(head):
+        for source, (_, _, _, odd) in enumerate(jobs):
             for owner in range(2):
 
                 @pl.when(odd == owner)
-                def _(head=head, source=source, owner=owner):
+                def _(source=source, owner=owner):
                     key_copy(source, head, owner).start()
                     value_copy(source, head, owner).start()
 
+    for source, (hops, _, _, _) in enumerate(jobs):
+        for place in range(places):
+            pl.when(jnp.minimum(hops, places - 1) == place)(query_copy(source, place).start)
+    start_head(0)
     mark_blocks(marks)
     for source in range(sources):
         count = rows // BLOCK
@@ -249,6 +250,8 @@
     key_copy(1, 0, 0).wait()
     for source in range(sources):
         value_copy(source, 0, 0).wait()
+    for head in range(1, heads):
+        start_head(head)
     lax.fori_loop(0, heads * pairs, one_pair, peaks)
     copies = []
     last = places - 1
@@ -372,21 +375,20 @@
             stat_ref[0, :, columns] = stats[:, j * BLOCK : (j + 1) * BLOCK]
 
 
-def attend_local(queries, keys, turned_values, bias, spots):
+def attend_local(queries, keys, turned_values, bias, spots, head, count):
     tokens = keys.shape[0]
     tile = min(256, tokens)
     blocks = bias.shape[1]
-    count = turned_values.shape[0]
     return kernel_call(
         functools.partial(local_body, tile=tile, spots=spots),
         "attend_local",
-        18,
+        10,
         grid=(count,),
         in_specs=[
-            pl.BlockSpec((tokens, LANES), lambda h: (0, h)),
-            pl.BlockSpec((tokens, LANES), lambda h: (0, h)),
-            pl.BlockSpec((1, LANES + STAT_ROWS, tokens), lambda h: (h, 0, 0)),
-            pl.BlockSpec((1, blocks, LANES), lambda h: (h, 0, 0)),
+            pl.BlockSpec((tokens, LANES), lambda h: (0, head + h)),
+            pl.BlockSpec((tokens, LANES), lambda h: (0, head + h)),
+            pl.BlockSpec((1, LANES + STAT_ROWS, tokens), lambda h: (head + h, 0, 0)),
+            pl.BlockSpec((1, blocks, LANES), lambda h: (head + h, 0, 0)),
         ],
         out_specs=[
             pl.BlockSpec((LANES, tokens), lambda h: (h, 0)),
@@ -445,61 +447,63 @@
     return kernel_call(
         functools.partial(merge_far_body, heads=heads, hops=hops),
         "merge_far",
-        2.3,
+        40,
         in_specs=[pl.BlockSpec(memory_space=pltpu.SMEM)] + [in_vmem] * len(pieces),
         out_specs=in_vmem,
         out_shape=jax.ShapeDtypeStruct(pieces[0].shape, jnp.bfloat16),
     )(info, *pieces)
 
 
-def merge_local_body(info_ref, normal_ref, stat_ref, *refs, heads, stages):
-    held_refs, out_ref = refs[:-1], refs[-1]
+def merge_local_body(info_ref, *refs, heads, runs, stages, groups):
+    local_refs, held_refs = refs[: 2 * runs], refs[2 * runs : -1 - groups]
+    out_refs, turned_ref = refs[-1 - groups : -1], refs[-1]
+    per_run = heads // runs
     others = len(held_refs) // stages
-    groups, _, columns = out_ref.shape
-    wide = columns // stages
+    wide = out_refs[0].shape[0] // stages
     flags = merge_flags(info_ref, 0)
-    slots = []
-    for piece in range(groups):
-        apart = info_ref[1] ^ piece
-        slots.append(jnp.where(info_ref[0] & 1 == 1, bit_reverse(apart, groups.bit_length() - 1), apart))
     for stage in range(stages):
         lanes = slice(stage * groups * wide, (stage + 1) * groups * wide)
         here = held_refs[stage * others : (stage + 1) * others]
         far_stats = [packed_stats(ref, heads) for ref in here]
         for head in range(heads):
             rows = slice(head * LANES, (head + 1) * LANES)
-            stat = sum(stat_ref[head, p : p + 1, lanes].astype(jnp.float32) for p in range(3))
-            pieces = [(normal_ref[rows, lanes], stat)]
+            normal_ref, stat_ref = local_refs[2 * (head // per_run) : 2 * (head // per_run) + 2]
+            spot = head % per_run
+            stat = sum(stat_ref[spot, p : p + 1, lanes].astype(jnp.float32) for p in range(3))
+            pieces = [(normal_ref[spot * LANES : (spot + 1) * LANES, lanes], stat)]
             pieces += [
                 (ref[rows, :], jnp.where(flag, far_stat[head], NEG_FILL))
                 for ref, far_stat, flag in zip(here, far_stats, flags)
             ]
-            held, _ = merge_many(pieces)
-            for piece in range(groups):
-                out_ref[slots[piece], rows, stage * wide : (stage + 1) * wide] = held[
-                    :, piece * wide : (piece + 1) * wide
-                ]
+            turned_ref[:, rows] = merge_many(pieces)[0].T
+        for place, out_ref in enumerate(out_refs):
+            apart = jnp.where(info_ref[0] & 1 == 1, bit_reverse(place, groups.bit_length() - 1), place)
+            first = pl.multiple_of((info_ref[1] ^ apart) * wide, wide)
+            out_ref[stage * wide : (stage + 1) * wide, :] = turned_ref[pl.ds(first, wide), :]
 
 
 def merge_local(info, local, first, stages, chunks, pieces, heads, groups):
-    normal, stat = local
-    columns = normal.shape[1] // chunks * stages
+    columns = local[0][0].shape[1] // chunks * stages
     assert first % stages == 0
-    specs = [
-        pl.BlockSpec(memory_space=pltpu.SMEM),
-        pl.BlockSpec((normal.shape[0], columns), lambda i: (0, first // stages)),
-        pl.BlockSpec((*stat.shape[:2], columns), lambda i: (0, 0, first // stages)),
-    ]
+    specs = [pl.BlockSpec(memory_space=pltpu.SMEM)]
+    for normal, stat in local:
+        specs += [
+            pl.BlockSpec((normal.shape[0], columns), lambda i: (0, first // stages)),
+            pl.BlockSpec((*stat.shape[:2], columns), lambda i: (0, 0, first // stages)),
+        ]
     specs += [pl.BlockSpec(piece.shape, lambda i: (0, 0)) for piece in pieces]
     return kernel_call(
-        functools.partial(merge_local_body, heads=heads, stages=stages),
+        functools.partial(
+            merge_local_body, heads=heads, runs=len(local), stages=stages, groups=groups
+        ),
         "merge_local",
-        4,
+        40,
         grid=(1,),
         in_specs=specs,
-        out_specs=pl.BlockSpec((groups, heads * LANES, columns // groups), lambda i: (0, 0, 0)),
-        out_shape=jax.ShapeDtypeStruct((groups, heads * LANES, columns // groups), jnp.bfloat16),
-    )(info, normal, stat, *pieces)
+        out_specs=[pl.BlockSpec((columns // groups, heads * LANES), lambda i: (0, 0))] * groups,
+        out_shape=[jax.ShapeDtypeStruct((columns // groups, heads * LANES), jnp.bfloat16)] * groups,
+        scratch_shapes=[pltpu.VMEM((columns // stages, heads * LANES), jnp.bfloat16)],
+    )(info, *[array for both in local for array in both], *pieces)
 
 
 def bit_reverse(place, bits):
@@ -510,7 +514,7 @@
     bits = sources.bit_length() - 1
     own_refs, other_refs = refs[: sources - 1], refs[sources - 1 : 2 * sources - 2]
     part_refs = refs[2 * sources - 2 : 2 * sources - 2 + stages * sources]
-    out_ref, held, sems = refs[-3:]
+    out_ref, held, outs, sems, out_sems = refs[-5:]
     depth, columns = weight_ref.shape
     half = depth // 2
     width = columns // cuts
@@ -533,22 +537,29 @@
         for copy in copies[-1]:
             copy.start()
     rows = [
-        jnp.concatenate([part_refs[stage * sources + place][...].T for place in range(sources)], 1)
+        jnp.concatenate([part_refs[stage * sources + place][...] for place in range(sources)], 1)
         for stage in range(stages)
     ]
     left = jnp.concatenate(rows, 0)
+    out_copies = []
     for cut in range(cuts):
         for copy in copies[cut]:
             copy.wait()
-        out_ref[:, cut * width : (cut + 1) * width] = jnp.dot(
-            left, held[cut], preferred_element_type=jnp.float32
-        ).astype(jnp.bfloat16)
+        outs[cut] = jnp.dot(left, held[cut], preferred_element_type=jnp.float32).astype(jnp.bfloat16)
+        out_copies.append(
+            pltpu.make_async_copy(
+                outs.at[cut], out_ref.at[:, cut * width : (cut + 1) * width], out_sems.at[cut]
+            )
+        )
+        out_copies[-1].start()
+    for copy in out_copies:
+        copy.wait()
 
 
 def project(info, weight_rows, own, other, parts):
     sources, stages, cuts = len(parts[0]), len(parts), 4
     depth, columns = weight_rows.shape
-    rows = sum(row[0].shape[1] for row in parts)
+    rows = sum(row[0].shape[0] for row in parts)
     anywhere, in_vmem = pl.BlockSpec(memory_space=pl.ANY), pl.BlockSpec(memory_space=pltpu.VMEM)
     flat = [piece for row in parts for piece in row]
     return kernel_call(
@@ -558,11 +569,13 @@
         in_specs=[pl.BlockSpec(memory_space=pltpu.SMEM)]
         + [anywhere] * (2 * sources - 1)
         + [in_vmem] * len(flat),
-        out_specs=in_vmem,
+        out_specs=anywhere,
         out_shape=jax.ShapeDtypeStruct((rows, columns), jnp.bfloat16),
         scratch_shapes=[
             pltpu.VMEM((cuts, sources * depth, columns // cuts), jnp.bfloat16),
+            pltpu.VMEM((cuts, rows, columns // cuts), jnp.bfloat16),
             pltpu.SemaphoreType.DMA((cuts, 2 * sources - 1)),
+            pltpu.SemaphoreType.DMA((cuts,)),
         ],
     )(info, weight_rows, *own, *other, *flat)
 
@@ -584,16 +597,16 @@
     return lax.ppermute(value, ("ctx", "head"), pairs)
 
 
-def gather_weights(weight_rows, parity, earlier):
-    count = lax.axis_size("head")
-    bits = count.bit_length() - 1
+def start_weights(weight_rows, parity, *earlier):
     half = weight_rows.shape[0] // 2
-    weight_rows = after(weight_rows, earlier[0])
-    held = [lax.dynamic_slice_in_dim(weight_rows, parity * half, half, 0)]
-    for number in range(bits):
-        sent = [after(piece, earlier[min(number, 1)]) for piece in held]
-        held += [swap_head(piece, 1 << number, 1 << (bits - 1 - number)) for piece in sent]
-    return held[1:], [swap_sibling(after(piece, earlier[2])) for piece in held[1:]]
+    return [lax.dynamic_slice_in_dim(after(weight_rows, *earlier), parity * half, half, 0)]
+
+
+def double_weights(held, *earlier):
+    bits = lax.axis_size("head").bit_length() - 1
+    number = len(held).bit_length() - 1
+    sent = [after(piece, *earlier) for piece in held]
+    return held + [swap_head(piece, 1 << number, 1 << (bits - 1 - number)) for piece in sent]
 
 
 def after(value, *earlier):
@@ -645,18 +658,21 @@
         moving = after(hops[number][-1], *earlier)
         hops[number].append(shift(moving, -2, 2, count - 2 * (done - 1)))
 
-    for number in range(min(3, chunks)):
+    for number in range(min(2, chunks)):
         move_down(number)
     keys = flat(key_states)
     turned_values, local_bias, *biases = prepare(info, flat(value_states), block_pattern, spots)
     both_keys = [keys, swap_sibling(keys)]
     both_values = [turned_values, swap_sibling(turned_values)]
-    local = attend_local(flat(query_states), keys, turned_values, local_bias, spots)
-    for number in range(3, chunks):
-        move_down(number, hops[number - 3][1])
+    queries = flat(query_states)
+    half = heads // 2
     for _ in range(1, places):
-        for number in range(chunks):
-            move_down(number)
+        move_down(0)
+    local = [attend_local(queries, keys, turned_values, local_bias, spots, 0, half)]
+    queries = after(queries, local[0][0], hops[0][-1])
+    local.append(attend_local(queries, keys, turned_values, local_bias, spots, half, half))
+    for number in range(2, chunks):
+        move_down(number, local[number % 2][0])
 
     def attend(number, *earlier):
         arrays = [*hops[number][:-1], after(hops[number][-1], *earlier)]
@@ -669,29 +685,41 @@
         pieces = [piece for number in range(first, first + stages) for piece in (moved[number], *own[number])]
         pieces[0] = after(pieces[0], *earlier)
         merged = merge_local(info, local, first, stages, chunks, pieces, heads, groups)
-        return merged, exchange(merged)
+        return merged[0], exchange(merged)
 
     own, moved, parts = {}, {}, []
-    last = local[0]
-    weights = None
+    last = local[1][0]
+    held = double_weights(start_weights(weight_rows, parity, hops[0][1]))
+    waits = {0: held[1:]}
+    while len(held) < groups:
+        first = len(held)
+        held = double_weights(held)
+        waits[1], waits[3] = waits.get(1, []) + held[first : first + 1], held[first + 1 :]
+    other = [swap_sibling(piece) for piece in held[1:]]
     for slot in range(chunks + places - 1):
+        for number in [1, 2] if slot == 0 else [slot + 2]:
+            for _ in range(1, places if number < chunks else 1):
+                move_down(number, last)
         if slot < chunks:
-            *own[slot], last = attend(slot, last)
+            arrived = waits.get(slot, [])
+            *own[slot], last = attend(slot, last, *arrived)
             moved[slot] = move_up(last, places)
-            if slot == min(1, chunks - 1):
-                weights = gather_weights(weight_rows, parity, [local[0], own[0][0], last])
         for behind in range(1, places):
             number = slot - behind
             if 0 <= number < chunks:
-                pieces = [after(moved[number], last), *own[number]]
+                waited = [moved[number - 1]] if 0 < number < chunks - 1 else []
+                pieces = [after(moved[number], last, *waited), *own[number]]
                 last = merge_far(info, pieces, heads, places - behind)
                 moved[number] = move_up(last, places - behind)
-    if chunks > 1:
-        last, exchanged = finish(0, chunks - 1, last)
+                if number == chunks - 2 and chunks == 4 and places == 2:
+                    last, exchanged = finish(0, 2, last)
+                    parts.append(exchanged)
+    done = sum(row[0].shape[0] for row in parts) * chunks * groups // tokens
+    for number in range(done, chunks):
+        waited = [*(parts[-1] if parts else []), *(other if number == done else [])]
+        last, exchanged = finish(number, 1, last, *waited)
         parts.append(exchanged)
-    last, exchanged = finish(chunks - 1, 1, last)
-    parts.append(exchanged)
-    return project(info, weight_rows, *weights, parts)
+    return project(info, weight_rows, held[1:], other, parts)
 
 
 def solution(mesh):

time: 271 us -> 226 us (0.83)
  waiting for transfers between devices: 73.1 us -> 32 us
  Pallas kernels: 126 us -> 121 us
  starting transfers between devices: 52.3 us -> 55.8 us
  local copies, waits for them, and re-layouts: 17.6 us -> 14.4 us
    ppermute x16, waiting for transfers between devices: 49.4 us -> 16.3 us  [shift(): lax.ppermute(value, 'ctx', [(source, source + steps) for source in range(...]
    ppermute x9 -> x12, waiting for transfers between devices: 23.7 us -> 15.7 us  [swap_head(): return lax.ppermute(value, ('ctx', 'head'), pairs)]
    pallas_call x4, Pallas kernels: 68.1 us -> 60.8 us  [attend_far(): kernel_call(functools.partial(far_body, places=len(queries), tile=tile, s...]
    ppermute x9 -> x12, starting transfers between devices: 11.7 us -> 16.1 us  [swap_head(): return lax.ppermute(value, ('ctx', 'head'), pairs)]
    squeeze x2 -> x0, local copies, waits for them, and re-layouts: 2.71 us -> none  [exchange(): pieces[place]]
    pallas_call x1 -> x2, Pallas kernels: 18.2 us -> 20.4 us  [attend_local(): kernel_call(functools.partial(local_body, tile=tile, spots=spots), 'atten...]
    pallas_call x2 -> x3, Pallas kernels: 9.16 us -> 10.9 us  [merge_local(): kernel_call(functools.partial(merge_local_body, heads=heads, runs=len(loc...]
    unnamed x49 -> x55, local copies, waits for them, and re-layouts: 10.8 us -> 9.5 us
  transfers between devices with their start and end apart: 30 -> 33, of which waited for: 12 -> 11; matrix products, arithmetic and copies ran while one was open for 4% -> 4% of each run, Pallas kernels for 41% -> 46%
where the time goes in v2:
time: 226 us; the launch traced here: 225 us
  Pallas kernels  121 us (54%)
  starting transfers between devices  55.8 us (25%)
  waiting for transfers between devices  32 us (14%)
  local copies, waits for them, and re-layouts  14.4 us (6%)
    pallas_call x4, Pallas kernels, attend_far(): kernel_call(functools.partial(far_body, places=len(queries), tile=tile, s...  60.8 us
    ppermute x16, starting transfers between devices, shift(): lax.ppermute(value, 'ctx', [(source, source + steps) for source in range(...  38.9 us
    pallas_call x2, Pallas kernels, attend_local(): kernel_call(functools.partial(local_body, tile=tile, spots=spots), 'atten...  20.4 us
    ppermute x16, waiting for transfers between devices, shift(): lax.ppermute(value, 'ctx', [(source, source + steps) for source in range(...  16.3 us
    ppermute x12, starting transfers between devices, swap_head(): return lax.ppermute(value, ('ctx', 'head'), pairs)  16.1 us
    ppermute x12, waiting for transfers between devices, swap_head(): return lax.ppermute(value, ('ctx', 'head'), pairs)  15.7 us
    pallas_call x1, Pallas kernels, project(): kernel_call(functools.partial(project_body, sources=sources, stages=stage...  14.3 us
    pallas_call x3, Pallas kernels, merge_local(): kernel_call(functools.partial(merge_local_body, heads=heads, runs=len(loc...  10.9 us
  transfers between devices with their start and end apart: 33, of which 11 were waited for; matrix products, arithmetic and copies ran while one was open for 4% of the time, Pallas kernels for 46%

profile of v2, /device:TPU:0, one launch (start us, length us, event | category | flops | bytes accessed | tf_op | source)
XLA Modules:
  0.0 225.0 jit_solution(5425330260960379607)
XLA Ops:
  0.0 3.2 %fusion = (bf16[4,1,128,4,128]{4,3,2,1,0:T(4,128)(2,1)S(1)}, bf16[4,1,128,4,128]{4,3,2,1,0:T(4,128)(2,1)S(1)}, bf16[4,1,128,4,128]{4,3,2,1,0:T(4,128)(2,1)}, bf16[4,1,128,4,128]{4,3,2,1,0:T(4,128)(2,1)S(1)}) fusion(bf16[4,4,128,4,128]{4,3,2,1,0:T(4,128)(2,1)} %bitcast.36), kind=kLoop, calls=%fused_computation.9 | loop fusion | bytes 4194304 | tf_op jit(solution)/shard_map/slice | solution.py:620
  7.7 4.4 %prepare.1 = (bf16[4,144,2048]{2,1,0:T(8,128)(2,1)}, f32[4,16,128]{2,1,0:T(8,128)}, f32[4,16,128]{2,1,0:T(8,128)}, f32[4,16,128]{2,1,0:T(8,128)}) custom-call(s32[4]{0:T(128)} %pad_add_fusion.info_ref, bf16[2048,512]{1,0:T(8,128)(2,1)} %bitcast.42, s32[4,128,128]{2,1,0:T(8,128)} %pattern_ref.1), custom_call_target="tpu_custom_call" | custom-call | flops 4600000000 | bytes 1 | tf_op jit(solution)/shard_map/prepare/pallas_call | solution.py:80
  18.4 2.9 %collective-permute-done.refs_1_ = bf16[512,512]{1,0:T(8,128)(2,1)} collective-permute-done((bf16[512,512]{1,0:T(8,128)(2,1)}, bf16[512,512]{1,0:T(8,128)(2,1)}, u32[]{:S(2)}, u32[]{:S(2)}) %collective-permute-start) | collective-permute-done | bytes 524320 | tf_op jit(solution)/shard_map/ppermute | solution.py:584
  26.0 10.2 %attend_local.2 = (bf16[256,2048]{1,0:T(8,128)(2,1)}, bf16[2,16,2048]{2,1,0:T(8,128)(2,1)}) custom-call(bf16[2048,512]{1,0:T(8,128)(2,1)} %bitcast.40, bf16[2048,512]{1,0:T(8,128)(2,1)} %bitcast.30.key_ref.refs_3_, bf16[4,144,2048]{2,1,0:T(8,128)(2,1)} %get-tuple-element.56.value_ref.refs_5_, f32[4,16,128]{2,1,0:T(8,128)} %get-tuple-element.57.bias_ref), custom_call_target="tpu_custom_call" | custom-call | flops 11500000256 | bytes 1 | tf_op jit(solution)/shard_map/attend_local/pallas_call | solution.py:382
  36.4 8.2 %collective-permute-done.7.refs_2_ = bf16[512,512]{1,0:T(8,128)(2,1)} collective-permute-done((bf16[512,512]{1,0:T(8,128)(2,1)}, bf16[512,512]{1,0:T(8,128)(2,1)}, u32[]{:S(2)}, u32[]{:S(2)}) %collective-permute-start.7) | collective-permute-done | bytes 524320 | tf_op jit(solution)/shard_map/ppermute | solution.py:584
  47.8 10.2 %attend_local.3 = (bf16[256,2048]{1,0:T(8,128)(2,1)}, bf16[2,16,2048]{2,1,0:T(8,128)(2,1)}) custom-call(bf16[2048,512]{1,0:T(8,128)(2,1)} %bitcast.41, bf16[2048,512]{1,0:T(8,128)(2,1)} %bitcast.30.key_ref.refs_3_, bf16[4,144,2048]{2,1,0:T(8,128)(2,1)} %get-tuple-element.56.value_ref.refs_5_, f32[4,16,128]{2,1,0:T(8,128)} %get-tuple-element.57.bias_ref), custom_call_target="tpu_custom_call" | custom-call | flops 11500000256 | bytes 1 | tf_op jit(solution)/shard_map/attend_local/pallas_call | solution.py:382
  58.0 2.1 collective-permute-done.14.refs_1_
  64.2 15.2 %attend_far.4 = (bf16[528,512]{1,0:T(8,128)(2,1)}, bf16[528,512]{1,0:T(8,128)(2,1)}, bf16[528,512]{1,0:T(8,128)(2,1)}) custom-call(s32[4]{0:T(128)} %pad_add_fusion.info_ref, bf16[512,512]{1,0:T(8,128)(2,1)} %bitcast.35.refs_0_, bf16[512,512]{1,0:T(8,128)(2,1)} %collective-permute-done.refs_1_, bf16[512,512]{1,0:T(8,128)(2,1)} %collective-permute-done.7.refs_2_, ...), custom_call_target="tpu_custom_call" | custom-call | flops 18400000000 | bytes 1 | tf_op jit(solution)/shard_map/attend_far/pallas_call | solution.py:303
  79.4 6.6 %collective-permute-start.10 = (bf16[528,512]{1,0:T(8,128)(2,1)}, bf16[528,512]{1,0:T(8,128)(2,1)}, u32[]{:S(2)}, u32[]{:S(2)}) collective-permute-start(bf16[528,512]{1,0:T(8,128)(2,1)} %get-tuple-element.66), channel_id=1, source_target_pairs={{0,8},{4,12},{8,16},{12,20},{1,9},{5,13},{9,17},{13,21},{2,10},{6,... | collective-permute-start | bytes 1622024 | tf_op jit(solution)/shard_map/ppermute | solution.py:584
  86.8 15.1 %attend_far.5 = (bf16[528,512]{1,0:T(8,128)(2,1)}, bf16[528,512]{1,0:T(8,128)(2,1)}, bf16[528,512]{1,0:T(8,128)(2,1)}) custom-call(s32[4]{0:T(128)} %pad_add_fusion.info_ref, bf16[512,512]{1,0:T(8,128)(2,1)} %bitcast.34.refs_0_, bf16[512,512]{1,0:T(8,128)(2,1)} %collective-permute-done.11.refs_1_, bf16[512,512]{1,0:T(8,128)(2,1)} %copy-done.14, ...), custom_call_target="tpu_custom_call" | custom-call | flops 18400000000 | bytes 1 | tf_op jit(solution)/shard_map/attend_far/pallas_call | solution.py:303
  102.0 4.0 %collective-permute-start.19 = (bf16[528,512]{1,0:T(8,128)(2,1)}, bf16[528,512]{1,0:T(8,128)(2,1)S(1)}, u32[]{:S(2)}, u32[]{:S(2)}) collective-permute-start(bf16[528,512]{1,0:T(8,128)(2,1)} %get-tuple-element.69), channel_id=1, source_target_pairs={{0,8},{4,12},{8,16},{12,20},{1,9},{5,13},{9,17},{13,21},{2,10},{6,... | collective-permute-start | bytes 1622024 | tf_op jit(solution)/shard_map/ppermute | solution.py:584
  109.0 2.6 %merge_far.4 = bf16[528,512]{1,0:T(8,128)(2,1)} custom-call(s32[4]{0:T(128)} %pad_add_fusion.info_ref, bf16[528,512]{1,0:T(8,128)(2,1)} %collective-permute-done.10.refs_0_, bf16[528,512]{1,0:T(8,128)(2,1)} %get-tuple-element.71.refs_1_.refs_5_, bf16[528,512]{1,0:T(8,128)(2,1)} %get-tuple-element.72.refs_2_.refs_6_), custom_call_target="tpu_custom_call" | custom-call | flops 46000001024 | bytes 1 | tf_op jit(solution)/shard_map/merge_far/pallas_call | solution.py:447
  111.6 4.6 %collective-permute-start.13 = (bf16[528,512]{1,0:T(8,128)(2,1)}, bf16[528,512]{1,0:T(8,128)(2,1)S(1)}, u32[]{:S(2)}, u32[]{:S(2)}) collective-permute-start(bf16[528,512]{1,0:T(8,128)(2,1)} %merge_far.4), channel_id=1, source_target_pairs={{0,8},{4,12},{8,16},{12,20},{16,24},{20,28},{1,9},{5,13},{9,17},{1... | collective-permute-start | bytes 1622024 | tf_op jit(solution)/shard_map/ppermute | solution.py:584
  116.2 15.2 %attend_far.6 = (bf16[528,512]{1,0:T(8,128)(2,1)}, bf16[528,512]{1,0:T(8,128)(2,1)}, bf16[528,512]{1,0:T(8,128)(2,1)}) custom-call(s32[4]{0:T(128)} %pad_add_fusion.info_ref, bf16[512,512]{1,0:T(8,128)(2,1)} %bitcast.52, bf16[512,512]{1,0:T(8,128)(2,1)} %collective-permute-done.14.refs_1_, bf16[512,512]{1,0:T(8,128)(2,1)} %collective-permute-done.15.refs_2_, ...), custom_call_target="tpu_custom_call" | custom-call | flops 18400000000 | bytes 1 | tf_op jit(solution)/shard_map/attend_far/pallas_call | solution.py:303
  131.7 3.4 %collective-permute-start.16 = (bf16[528,512]{1,0:T(8,128)(2,1)}, bf16[528,512]{1,0:T(8,128)(2,1)}, u32[]{:S(2)}, u32[]{:S(2)}) collective-permute-start(bf16[528,512]{1,0:T(8,128)(2,1)} %get-tuple-element.76), channel_id=1, source_target_pairs={{0,8},{4,12},{8,16},{12,20},{1,9},{5,13},{9,17},{13,21},{2,10},{6,... | collective-permute-start | bytes 1622024 | tf_op jit(solution)/shard_map/ppermute | solution.py:584
  135.1 2.6 %merge_far.5 = bf16[528,512]{1,0:T(8,128)(2,1)} custom-call(s32[4]{0:T(128)} %pad_add_fusion.info_ref, bf16[528,512]{1,0:T(8,128)(2,1)} %copy-done.12, bf16[528,512]{1,0:T(8,128)(2,1)} %get-tuple-element.80.refs_1_.refs_8_, bf16[528,512]{1,0:T(8,128)(2,1)} %get-tuple-element.81.refs_2_.refs_9_), custom_call_target="tpu_custom_call" | custom-call | flops 46000001024 | bytes 1 | tf_op jit(solution)/shard_map/merge_far/pallas_call | solution.py:447
  139.1 15.3 %attend_far.7 = (bf16[528,512]{1,0:T(8,128)(2,1)}, bf16[528,512]{1,0:T(8,128)(2,1)}, bf16[528,512]{1,0:T(8,128)(2,1)}) custom-call(s32[4]{0:T(128)} %pad_add_fusion.info_ref, bf16[512,512]{1,0:T(8,128)(2,1)} %bitcast.50, bf16[512,512]{1,0:T(8,128)(2,1)} %collective-permute-done.17.refs_1_, bf16[512,512]{1,0:T(8,128)(2,1)} %collective-permute-done.18.refs_2_, ...), custom_call_target="tpu_custom_call" | custom-call | flops 18400000000 | bytes 1 | tf_op jit(solution)/shard_map/attend_far/pallas_call | solution.py:303
  156.4 2.3 %collective-permute-done.20.refs_7_ = bf16[528,512]{1,0:T(8,128)(2,1)S(1)} collective-permute-done((bf16[528,512]{1,0:T(8,128)(2,1)}, bf16[528,512]{1,0:T(8,128)(2,1)S(1)}, u32[]{:S(2)}, u32[]{:S(2)}) %collective-permute-start.20) | collective-permute-done | bytes 540704 | tf_op jit(solution)/shard_map/ppermute | solution.py:584
  158.8 2.9 %merge_far.6 = bf16[528,512]{1,0:T(8,128)(2,1)} custom-call(s32[4]{0:T(128)} %pad_add_fusion.info_ref, bf16[528,512]{1,0:T(8,128)(2,1)} %collective-permute-done.16.refs_0_, bf16[528,512]{1,0:T(8,128)(2,1)} %get-tuple-element.85.refs_1_.refs_5_, bf16[528,512]{1,0:T(8,128)(2,1)} %get-tuple-element.86.refs_2_.refs_6_), custom_call_target="tpu_custom_call" | custom-call | flops 46000001024 | bytes 1 | tf_op jit(solution)/shard_map/merge_far/pallas_call | solution.py:447
  161.6 4.5 %collective-permute-start.24 = (bf16[528,512]{1,0:T(8,128)(2,1)}, bf16[528,512]{1,0:T(8,128)(2,1)S(1)}, u32[]{:S(2)}, u32[]{:S(2)}) collective-permute-start(bf16[528,512]{1,0:T(8,128)(2,1)} %merge_far.6), channel_id=1, source_target_pairs={{0,8},{4,12},{8,16},{12,20},{16,24},{20,28},{1,9},{5,13},{9,17},{1... | collective-permute-start | bytes 1622024 | tf_op jit(solution)/shard_map/ppermute | solution.py:584
  166.2 4.6 %merge_local.3 = (bf16[256,512]{1,0:T(8,128)(2,1)}, bf16[256,512]{1,0:T(8,128)(2,1)}, bf16[256,512]{1,0:T(8,128)(2,1)}, bf16[256,512]{1,0:T(8,128)(2,1)}) custom-call(s32[4]{0:T(128)} %pad_add_fusion.info_ref, bf16[256,2048]{1,0:T(8,128)(2,1)} %get-tuple-element.58.refs_0_, bf16[2,16,2048]{2,1,0:T(8,128)(2,1)} %get-tuple-element.59.refs_1_, ...), custom_call_target="tpu_custom_call" | custom-call | flops 46000001024 | bytes 1 | tf_op jit(solution)/shard_map/merge_local/pallas_call | solution.py:495
  174.3 2.6 %merge_far.7 = bf16[528,512]{1,0:T(8,128)(2,1)} custom-call(s32[4]{0:T(128)} %pad_add_fusion.info_ref, bf16[528,512]{1,0:T(8,128)(2,1)} %copy-done.11, bf16[528,512]{1,0:T(8,128)(2,1)} %get-tuple-element.93.refs_1_.refs_5_, bf16[528,512]{1,0:T(8,128)(2,1)} %get-tuple-element.94.refs_2_.refs_6_), custom_call_target="tpu_custom_call" | custom-call | flops 46000001024 | bytes 1 | tf_op jit(solution)/shard_map/merge_far/pallas_call | solution.py:447
  177.0 3.3 %collective-permute-done.21.refs_7_ = bf16[256,512]{1,0:T(8,128)(2,1)S(1)} collective-permute-done((bf16[256,512]{1,0:T(8,128)(2,1)}, bf16[256,512]{1,0:T(8,128)(2,1)S(1)}, u32[]{:S(2)}, u32[]{:S(2)}) %collective-permute-start.21) | collective-permute-done | bytes 262176 | tf_op jit(solution)/shard_map/ppermute | solution.py:597
  182.3 2.3 %collective-permute-done.23.refs_9_ = bf16[256,512]{1,0:T(8,128)(2,1)S(1)} collective-permute-done((bf16[256,512]{1,0:T(8,128)(2,1)}, bf16[256,512]{1,0:T(8,128)(2,1)S(1)}, u32[]{:S(2)}, u32[]{:S(2)}) %collective-permute-start.23) | collective-permute-done | bytes 262176 | tf_op jit(solution)/shard_map/ppermute | solution.py:597
  185.4 3.1 %merge_local.4 = (bf16[128,512]{1,0:T(8,128)(2,1)}, bf16[128,512]{1,0:T(8,128)(2,1)}, bf16[128,512]{1,0:T(8,128)(2,1)}, bf16[128,512]{1,0:T(8,128)(2,1)}) custom-call(s32[4]{0:T(128)} %pad_add_fusion.info_ref, bf16[256,2048]{1,0:T(8,128)(2,1)} %get-tuple-element.58.refs_0_, bf16[2,16,2048]{2,1,0:T(8,128)(2,1)} %get-tuple-element.59.refs_1_, ...), custom_call_target="tpu_custom_call" | custom-call | flops 46000001024 | bytes 1 | tf_op jit(solution)/shard_map/merge_local/pallas_call | solution.py:495
  192.9 2.1 collective-permute-done.26.refs_11_
  194.9 3.1 %collective-permute-done.27.refs_12_ = bf16[128,512]{1,0:T(8,128)(2,1)S(1)} collective-permute-done((bf16[128,512]{1,0:T(8,128)(2,1)}, bf16[128,512]{1,0:T(8,128)(2,1)S(1)}, u32[]{:S(2)}, u32[]{:S(2)}) %collective-permute-start.27) | collective-permute-done | bytes 131104 | tf_op jit(solution)/shard_map/ppermute | solution.py:597
  198.1 3.2 %merge_local.5 = (bf16[128,512]{1,0:T(8,128)(2,1)}, bf16[128,512]{1,0:T(8,128)(2,1)}, bf16[128,512]{1,0:T(8,128)(2,1)}, bf16[128,512]{1,0:T(8,128)(2,1)}) custom-call(s32[4]{0:T(128)} %pad_add_fusion.info_ref, bf16[256,2048]{1,0:T(8,128)(2,1)} %get-tuple-element.58.refs_0_, bf16[2,16,2048]{2,1,0:T(8,128)(2,1)} %get-tuple-element.59.refs_1_, ...), custom_call_target="tpu_custom_call" | custom-call | flops 46000001024 | bytes 1 | tf_op jit(solution)/shard_map/merge_local/pallas_call | solution.py:495
  202.4 2.5 %collective-permute-start.32 = (bf16[128,512]{1,0:T(8,128)(2,1)}, bf16[128,512]{1,0:T(8,128)(2,1)S(1)}, u32[]{:S(2)}, u32[]{:S(2)}) collective-permute-start(bf16[128,512]{1,0:T(8,128)(2,1)} %get-tuple-element.104), channel_id=1, source_target_pairs={{0,3},{1,2},{2,1},{3,0},{4,7},{5,6},{6,5},{7,4},{8,11},{9,10},{10,... | collective-permute-start | bytes 393224 | tf_op jit(solution)/shard_map/ppermute | solution.py:597
  204.9 2.8 %collective-permute-done.30.refs_15_ = bf16[128,512]{1,0:T(8,128)(2,1)S(1)} collective-permute-done((bf16[128,512]{1,0:T(8,128)(2,1)}, bf16[128,512]{1,0:T(8,128)(2,1)S(1)}, u32[]{:S(2)}, u32[]{:S(2)}) %collective-permute-start.30) | collective-permute-done | bytes 131104 | tf_op jit(solution)/shard_map/ppermute | solution.py:597
  207.7 2.1 collective-permute-done.31.refs_16_
  210.5 14.3 %project.1 = bf16[512,4096]{1,0:T(8,128)(2,1)} custom-call(s32[4]{0:T(128)} %pad_add_fusion.info_ref, bf16[512,4096]{1,0:T(8,128)(2,1)} %bitcast.48, bf16[256,4096]{1,0:T(8,128)(2,1)} %collective-permute-done.1.refs_0_, bf16[256,4096]{1,0:T(8,128)(2,1)} %collective-permute-done.2.refs_1_, bf16[256,4096]{1,0:T(8,128)(2,1)} %copy-done.7, ...), custom_call_target="tpu_custom_call" | custom-call | flops 17250000896 | bytes 1 | tf_op jit(solution)/shard_map/project/pallas_call | solution.py:565
  (107 shorter events, 43.0 us)
Async XLA Ops:
  4.1 17.2 %collective-permute-start = (bf16[512,512]{1,0:T(8,128)(2,1)}, bf16[512,512]{1,0:T(8,128)(2,1)}, u32[]{:S(2)}, u32[]{:S(2)}) collective-permute-start(bf16[512,512]{1,0:T(8,128)(2,1)} %bitcast.35.refs_0_), channel_id=1, source_target_pairs={{8,0},{12,4},{16,8},{20,12},{24,16},{28,20},{9,1},{13,5},{17,9},{2... | collective-permute-start | bytes 1572872 | tf_op jit(solution)/shard_map/ppermute | solution.py:584
  12.1 52.1 %collective-permute-start.9 = (bf16[4,144,2048]{2,1,0:T(8,128)(2,1)}, bf16[4,144,2048]{2,1,0:T(8,128)(2,1)}, u32[]{:S(2)}, u32[]{:S(2)}) collective-permute-start(bf16[4,144,2048]{2,1,0:T(8,128)(2,1)} %get-tuple-element.56.value_ref.refs_5_), channel_id=1, source_target_pairs={{0,4},{4,0},{8,12},{12,8},{16,20},{20,16},{24,28},{28,24},{1,5},{5... | collective-permute-start | bytes 7077896 | tf_op jit(solution)/shard_map/ppermute | solution.py:588
  14.3 48.4 %collective-permute-start.8 = (bf16[2048,512]{1,0:T(8,128)(2,1)}, bf16[2048,512]{1,0:T(8,128)(2,1)}, u32[]{:S(2)}, u32[]{:S(2)}) collective-permute-start(bf16[2048,512]{1,0:T(8,128)(2,1)} %bitcast.30.key_ref.refs_3_), channel_id=1, source_target_pairs={{0,4},{4,0},{8,12},{12,8},{16,20},{20,16},{24,28},{28,24},{1,5},{5... | collective-permute-start | bytes 6291464 | tf_op jit(solution)/shard_map/ppermute | solution.py:588
  15.3 30.5 %collective-permute-start.11 = (bf16[512,512]{1,0:T(8,128)(2,1)}, bf16[512,512]{1,0:T(8,128)(2,1)}, u32[]{:S(2)}, u32[]{:S(2)}) collective-permute-start(bf16[512,512]{1,0:T(8,128)(2,1)} %bitcast.34.refs_0_), channel_id=1, source_target_pairs={{8,0},{12,4},{16,8},{20,12},{24,16},{28,20},{9,1},{13,5},{17,9},{2... | collective-permute-start | bytes 1572872 | tf_op jit(solution)/shard_map/ppermute | solution.py:584
  21.2 23.3 %collective-permute-start.7 = (bf16[512,512]{1,0:T(8,128)(2,1)}, bf16[512,512]{1,0:T(8,128)(2,1)}, u32[]{:S(2)}, u32[]{:S(2)}) collective-permute-start(bf16[512,512]{1,0:T(8,128)(2,1)} %collective-permute-done.refs_1_), channel_id=1, source_target_pairs={{8,0},{12,4},{16,8},{20,12},{9,1},{13,5},{17,9},{21,13},{10,2},{14... | collective-permute-start | bytes 1572872 | tf_op jit(solution)/shard_map/ppermute | solution.py:584
  24.3 37.2 %collective-permute-start.1 = (bf16[256,4096]{1,0:T(8,128)(2,1)S(1)}, bf16[256,4096]{1,0:T(8,128)(2,1)}, u32[]{:S(2)}, u32[]{:S(2)}) collective-permute-start(bf16[256,4096]{1,0:T(8,128)(2,1)S(1)} %constant_dynamic-slice_fusion), channel_id=1, source_target_pairs={{0,1},{1,0},{2,3},{3,2},{4,6},{5,7},{6,4},{7,5},{8,9},{9,8},{10,11... | collective-permute-start | bytes 6291464 | tf_op jit(solution)/shard_map/ppermute | solution.py:597
  44.5 15.6 %collective-permute-start.14 = (bf16[512,512]{1,0:T(8,128)(2,1)S(1)}, bf16[512,512]{1,0:T(8,128)(2,1)}, u32[]{:S(2)}, u32[]{:S(2)}) collective-permute-start(bf16[512,512]{1,0:T(8,128)(2,1)S(1)} %bitcast.51), channel_id=1, source_target_pairs={{8,0},{12,4},{16,8},{20,12},{24,16},{28,20},{9,1},{13,5},{17,9},{2... | collective-permute-start | bytes 1572872 | tf_op jit(solution)/shard_map/ppermute | solution.py:584
  45.8 40.2 %collective-permute-start.2 = (bf16[256,4096]{1,0:T(8,128)(2,1)S(1)}, bf16[256,4096]{1,0:T(8,128)(2,1)}, u32[]{:S(2)}, u32[]{:S(2)}) collective-permute-start(bf16[256,4096]{1,0:T(8,128)(2,1)S(1)} %constant_dynamic-slice_fusion), channel_id=1, source_target_pairs={{0,2},{1,3},{2,0},{3,1},{4,5},{5,4},{6,7},{7,6},{8,10},{9,11},{10,... | collective-permute-start | bytes 6291464 | tf_op jit(solution)/shard_map/ppermute | solution.py:597
  60.1 25.9 %collective-permute-start.12 = (bf16[512,512]{1,0:T(8,128)(2,1)}, bf16[512,512]{1,0:T(8,128)(2,1)S(1)}, u32[]{:S(2)}, u32[]{:S(2)}) collective-permute-start(bf16[512,512]{1,0:T(8,128)(2,1)} %collective-permute-done.11.refs_1_), channel_id=1, source_target_pairs={{8,0},{12,4},{16,8},{20,12},{9,1},{13,5},{17,9},{21,13},{10,2},{14... | collective-permute-start | bytes 1572872 | tf_op jit(solution)/shard_map/ppermute | solution.py:584
  61.4 50.2 %collective-permute-start.15 = (bf16[512,512]{1,0:T(8,128)(2,1)}, bf16[512,512]{1,0:T(8,128)(2,1)}, u32[]{:S(2)}, u32[]{:S(2)}) collective-permute-start(bf16[512,512]{1,0:T(8,128)(2,1)} %collective-permute-done.14.refs_1_), channel_id=1, source_target_pairs={{8,0},{12,4},{16,8},{20,12},{9,1},{13,5},{17,9},{21,13},{10,2},{14... | collective-permute-start | bytes 1572872 | tf_op jit(solution)/shard_map/ppermute | solution.py:584
  62.7 43.2 %collective-permute-start.17 = (bf16[512,512]{1,0:T(8,128)(2,1)S(1)}, bf16[512,512]{1,0:T(8,128)(2,1)}, u32[]{:S(2)}, u32[]{:S(2)}) collective-permute-start(bf16[512,512]{1,0:T(8,128)(2,1)S(1)} %bitcast.49), channel_id=1, source_target_pairs={{8,0},{12,4},{16,8},{20,12},{24,16},{28,20},{9,1},{13,5},{17,9},{2... | collective-permute-start | bytes 1572872 | tf_op jit(solution)/shard_map/ppermute | solution.py:584
  79.4 29.6 %collective-permute-start.10 = (bf16[528,512]{1,0:T(8,128)(2,1)}, bf16[528,512]{1,0:T(8,128)(2,1)}, u32[]{:S(2)}, u32[]{:S(2)}) collective-permute-start(bf16[528,512]{1,0:T(8,128)(2,1)} %get-tuple-element.66), channel_id=1, source_target_pairs={{0,8},{4,12},{8,16},{12,20},{1,9},{5,13},{9,17},{13,21},{2,10},{6,... | collective-permute-start | bytes 1622024 | tf_op jit(solution)/shard_map/ppermute | solution.py:584
  102.0 29.4 %collective-permute-start.19 = (bf16[528,512]{1,0:T(8,128)(2,1)}, bf16[528,512]{1,0:T(8,128)(2,1)S(1)}, u32[]{:S(2)}, u32[]{:S(2)}) collective-permute-start(bf16[528,512]{1,0:T(8,128)(2,1)} %get-tuple-element.69), channel_id=1, source_target_pairs={{0,8},{4,12},{8,16},{12,20},{1,9},{5,13},{9,17},{13,21},{2,10},{6,... | collective-permute-start | bytes 1622024 | tf_op jit(solution)/shard_map/ppermute | solution.py:584
  105.9 31.7 %collective-permute-start.18 = (bf16[512,512]{1,0:T(8,128)(2,1)}, bf16[512,512]{1,0:T(8,128)(2,1)}, u32[]{:S(2)}, u32[]{:S(2)}) collective-permute-start(bf16[512,512]{1,0:T(8,128)(2,1)} %collective-permute-done.17.refs_1_), channel_id=1, source_target_pairs={{8,0},{12,4},{16,8},{20,12},{9,1},{13,5},{17,9},{21,13},{10,2},{14... | collective-permute-start | bytes 1572872 | tf_op jit(solution)/shard_map/ppermute | solution.py:584
  107.2 31.9 %collective-permute-start.3 = (bf16[256,4096]{1,0:T(8,128)(2,1)}, bf16[256,4096]{1,0:T(8,128)(2,1)S(1)}, u32[]{:S(2)}, u32[]{:S(2)}) collective-permute-start(bf16[256,4096]{1,0:T(8,128)(2,1)} %collective-permute-done.1.refs_0_), channel_id=1, source_target_pairs={{0,2},{1,3},{2,0},{3,1},{4,5},{5,4},{6,7},{7,6},{8,10},{9,11},{10,... | collective-permute-start | bytes 6291464 | tf_op jit(solution)/shard_map/ppermute | solution.py:597
  109.0 63.8 %collective-permute-start.4 = (bf16[256,4096]{1,0:T(8,128)(2,1)}, bf16[256,4096]{1,0:T(8,128)(2,1)}, u32[]{:S(2)}, u32[]{:S(2)}) collective-permute-start(bf16[256,4096]{1,0:T(8,128)(2,1)} %collective-permute-done.1.refs_0_), channel_id=1, source_target_pairs={{0,4},{4,0},{8,12},{12,8},{16,20},{20,16},{24,28},{28,24},{1,5},{5... | collective-permute-start | bytes 6291464 | tf_op jit(solution)/shard_map/ppermute | solution.py:588
  111.6 20.1 %collective-permute-start.13 = (bf16[528,512]{1,0:T(8,128)(2,1)}, bf16[528,512]{1,0:T(8,128)(2,1)S(1)}, u32[]{:S(2)}, u32[]{:S(2)}) collective-permute-start(bf16[528,512]{1,0:T(8,128)(2,1)} %merge_far.4), channel_id=1, source_target_pairs={{0,8},{4,12},{8,16},{12,20},{16,24},{20,28},{1,9},{5,13},{9,17},{1... | collective-permute-start | bytes 1622024 | tf_op jit(solution)/shard_map/ppermute | solution.py:584
  131.4 42.9 %collective-permute-start.5 = (bf16[256,4096]{1,0:T(8,128)(2,1)}, bf16[256,4096]{1,0:T(8,128)(2,1)}, u32[]{:S(2)}, u32[]{:S(2)}) collective-permute-start(bf16[256,4096]{1,0:T(8,128)(2,1)} %collective-permute-done.2.refs_1_), channel_id=1, source_target_pairs={{0,4},{4,0},{8,12},{12,8},{16,20},{20,16},{24,28},{28,24},{1,5},{5... | collective-permute-start | bytes 6291464 | tf_op jit(solution)/shard_map/ppermute | solution.py:588
  131.7 24.7 %collective-permute-start.16 = (bf16[528,512]{1,0:T(8,128)(2,1)}, bf16[528,512]{1,0:T(8,128)(2,1)}, u32[]{:S(2)}, u32[]{:S(2)}) collective-permute-start(bf16[528,512]{1,0:T(8,128)(2,1)} %get-tuple-element.76), channel_id=1, source_target_pairs={{0,8},{4,12},{8,16},{12,20},{1,9},{5,13},{9,17},{13,21},{2,10},{6,... | collective-permute-start | bytes 1622024 | tf_op jit(solution)/shard_map/ppermute | solution.py:584
  137.7 21.1 %collective-permute-start.20 = (bf16[528,512]{1,0:T(8,128)(2,1)}, bf16[528,512]{1,0:T(8,128)(2,1)S(1)}, u32[]{:S(2)}, u32[]{:S(2)}) collective-permute-start(bf16[528,512]{1,0:T(8,128)(2,1)} %merge_far.5), channel_id=1, source_target_pairs={{0,8},{4,12},{8,16},{12,20},{16,24},{20,28},{1,9},{5,13},{9,17},{1... | collective-permute-start | bytes 1622024 | tf_op jit(solution)/shard_map/ppermute | solution.py:584
  154.5 17.8 %collective-permute-start.25 = (bf16[528,512]{1,0:T(8,128)(2,1)}, bf16[528,512]{1,0:T(8,128)(2,1)S(1)}, u32[]{:S(2)}, u32[]{:S(2)}) collective-permute-start(bf16[528,512]{1,0:T(8,128)(2,1)} %get-tuple-element.83), channel_id=1, source_target_pairs={{0,8},{4,12},{8,16},{12,20},{1,9},{5,13},{9,17},{13,21},{2,10},{6,... | collective-permute-start | bytes 1622024 | tf_op jit(solution)/shard_map/ppermute | solution.py:584
  161.6 23.0 %collective-permute-start.24 = (bf16[528,512]{1,0:T(8,128)(2,1)}, bf16[528,512]{1,0:T(8,128)(2,1)S(1)}, u32[]{:S(2)}, u32[]{:S(2)}) collective-permute-start(bf16[528,512]{1,0:T(8,128)(2,1)} %merge_far.6), channel_id=1, source_target_pairs={{0,8},{4,12},{8,16},{12,20},{16,24},{20,28},{1,9},{5,13},{9,17},{1... | collective-permute-start | bytes 1622024 | tf_op jit(solution)/shard_map/ppermute | solution.py:584
  170.8 9.5 %collective-permute-start.21 = (bf16[256,512]{1,0:T(8,128)(2,1)}, bf16[256,512]{1,0:T(8,128)(2,1)S(1)}, u32[]{:S(2)}, u32[]{:S(2)}) collective-permute-start(bf16[256,512]{1,0:T(8,128)(2,1)} %get-tuple-element.89), channel_id=1, source_target_pairs={{0,1},{1,0},{2,3},{3,2},{4,6},{5,7},{6,4},{7,5},{8,9},{9,8},{10,11... | collective-permute-start | bytes 786440 | tf_op jit(solution)/shard_map/ppermute | solution.py:597
  172.3 10.0 %collective-permute-start.22 = (bf16[256,512]{1,0:T(8,128)(2,1)}, bf16[256,512]{1,0:T(8,128)(2,1)S(1)}, u32[]{:S(2)}, u32[]{:S(2)}) collective-permute-start(bf16[256,512]{1,0:T(8,128)(2,1)} %get-tuple-element.90), channel_id=1, source_target_pairs={{0,2},{1,3},{2,0},{3,1},{4,5},{5,4},{6,7},{7,6},{8,10},{9,11},{10,... | collective-permute-start | bytes 786440 | tf_op jit(solution)/shard_map/ppermute | solution.py:597
  172.8 11.8 %collective-permute-start.23 = (bf16[256,512]{1,0:T(8,128)(2,1)}, bf16[256,512]{1,0:T(8,128)(2,1)S(1)}, u32[]{:S(2)}, u32[]{:S(2)}) collective-permute-start(bf16[256,512]{1,0:T(8,128)(2,1)} %get-tuple-element.91), channel_id=1, source_target_pairs={{0,3},{1,2},{2,1},{3,0},{4,7},{5,6},{6,5},{7,4},{8,11},{9,10},{10,... | collective-permute-start | bytes 786440 | tf_op jit(solution)/shard_map/ppermute | solution.py:597
  174.3 10.3 %collective-permute-start.6 = (bf16[256,4096]{1,0:T(8,128)(2,1)S(1)}, bf16[256,4096]{1,0:T(8,128)(2,1)}, u32[]{:S(2)}, u32[]{:S(2)}) collective-permute-start(bf16[256,4096]{1,0:T(8,128)(2,1)S(1)} %collective-permute-done.3.refs_2_), channel_id=1, source_target_pairs={{0,4},{4,0},{8,12},{12,8},{16,20},{20,16},{24,28},{28,24},{1,5},{5... | collective-permute-start | bytes 6291464 | tf_op jit(solution)/shard_map/ppermute | solution.py:588
  180.3 12.6 %collective-permute-start.29 = (bf16[528,512]{1,0:T(8,128)(2,1)}, bf16[528,512]{1,0:T(8,128)(2,1)S(1)}, u32[]{:S(2)}, u32[]{:S(2)}) collective-permute-start(bf16[528,512]{1,0:T(8,128)(2,1)} %merge_far.7), channel_id=1, source_target_pairs={{0,8},{4,12},{8,16},{12,20},{16,24},{20,28},{1,9},{5,13},{9,17},{1... | collective-permute-start | bytes 1622024 | tf_op jit(solution)/shard_map/ppermute | solution.py:584
  188.5 6.4 %collective-permute-start.26 = (bf16[128,512]{1,0:T(8,128)(2,1)}, bf16[128,512]{1,0:T(8,128)(2,1)S(1)}, u32[]{:S(2)}, u32[]{:S(2)}) collective-permute-start(bf16[128,512]{1,0:T(8,128)(2,1)} %get-tuple-element.97), channel_id=1, source_target_pairs={{0,1},{1,0},{2,3},{3,2},{4,6},{5,7},{6,4},{7,5},{8,9},{9,8},{10,11... | collective-permute-start | bytes 393224 | tf_op jit(solution)/shard_map/ppermute | solution.py:597
  190.1 8.0 %collective-permute-start.27 = (bf16[128,512]{1,0:T(8,128)(2,1)}, bf16[128,512]{1,0:T(8,128)(2,1)S(1)}, u32[]{:S(2)}, u32[]{:S(2)}) collective-permute-start(bf16[128,512]{1,0:T(8,128)(2,1)} %get-tuple-element.98), channel_id=1, source_target_pairs={{0,2},{1,3},{2,0},{3,1},{4,5},{5,4},{6,7},{7,6},{8,10},{9,11},{10,... | collective-permute-start | bytes 393224 | tf_op jit(solution)/shard_map/ppermute | solution.py:597
  190.6 7.5 %collective-permute-start.28 = (bf16[128,512]{1,0:T(8,128)(2,1)}, bf16[128,512]{1,0:T(8,128)(2,1)S(1)}, u32[]{:S(2)}, u32[]{:S(2)}) collective-permute-start(bf16[128,512]{1,0:T(8,128)(2,1)} %get-tuple-element.99), channel_id=1, source_target_pairs={{0,3},{1,2},{2,1},{3,0},{4,7},{5,6},{6,5},{7,4},{8,11},{9,10},{10,... | collective-permute-start | bytes 393224 | tf_op jit(solution)/shard_map/ppermute | solution.py:597
  201.9 7.9 %collective-permute-start.31 = (bf16[128,512]{1,0:T(8,128)(2,1)}, bf16[128,512]{1,0:T(8,128)(2,1)S(1)}, u32[]{:S(2)}, u32[]{:S(2)}) collective-permute-start(bf16[128,512]{1,0:T(8,128)(2,1)} %get-tuple-element.103), channel_id=1, source_target_pairs={{0,2},{1,3},{2,0},{3,1},{4,5},{5,4},{6,7},{7,6},{8,10},{9,11},{10,... | collective-permute-start | bytes 393224 | tf_op jit(solution)/shard_map/ppermute | solution.py:597
  202.4 7.4 %collective-permute-start.32 = (bf16[128,512]{1,0:T(8,128)(2,1)}, bf16[128,512]{1,0:T(8,128)(2,1)S(1)}, u32[]{:S(2)}, u32[]{:S(2)}) collective-permute-start(bf16[128,512]{1,0:T(8,128)(2,1)} %get-tuple-element.104), channel_id=1, source_target_pairs={{0,3},{1,2},{2,1},{3,0},{4,7},{5,6},{6,5},{7,4},{8,11},{9,10},{10,... | collective-permute-start | bytes 393224 | tf_op jit(solution)/shard_map/ppermute | solution.py:597
  (25 other events, 163.5 us)

commit v3 on v2

--- a/solution.py
+++ b/solution.py
@@ -457,7 +457,9 @@
 def merge_local_body(info_ref, *refs, heads, runs, stages, groups):
     local_refs, held_refs = refs[: 2 * runs], refs[2 * runs : -1 - groups]
     out_refs, turned_ref = refs[-1 - groups : -1], refs[-1]
-    per_run = heads // runs
+    owners = [
+        (run, spot) for run in range(runs) for spot in range(local_refs[2 * run].shape[0] // LANES)
+    ]
     others = len(held_refs) // stages
     wide = out_refs[0].shape[0] // stages
     flags = merge_flags(info_ref, 0)
@@ -467,8 +469,8 @@
         far_stats = [packed_stats(ref, heads) for ref in here]
         for head in range(heads):
             rows = slice(head * LANES, (head + 1) * LANES)
-            normal_ref, stat_ref = local_refs[2 * (head // per_run) : 2 * (head // per_run) + 2]
-            spot = head % per_run
+            run, spot = owners[head]
+            normal_ref, stat_ref = local_refs[2 * run : 2 * run + 2]
             stat = sum(stat_ref[spot, p : p + 1, lanes].astype(jnp.float32) for p in range(3))
             pieces = [(normal_ref[spot * LANES : (spot + 1) * LANES, lanes], stat)]
             pieces += [
@@ -665,12 +667,12 @@
     both_keys = [keys, swap_sibling(keys)]
     both_values = [turned_values, swap_sibling(turned_values)]
     queries = flat(query_states)
-    half = heads // 2
+    early = heads - max(1, heads // 4)
     for _ in range(1, places):
         move_down(0)
-    local = [attend_local(queries, keys, turned_values, local_bias, spots, 0, half)]
+    local = [attend_local(queries, keys, turned_values, local_bias, spots, 0, early)]
     queries = after(queries, local[0][0], hops[0][-1])
-    local.append(attend_local(queries, keys, turned_values, local_bias, spots, half, half))
+    local.append(attend_local(queries, keys, turned_values, local_bias, spots, early, heads - early))
     for number in range(2, chunks):
         move_down(number, local[number % 2][0])
 
@@ -716,7 +718,9 @@
                     parts.append(exchanged)
     done = sum(row[0].shape[0] for row in parts) * chunks * groups // tokens
     for number in range(done, chunks):
-        waited = [*(parts[-1] if parts else []), *(other if number == done else [])]
+        waited = other if number == done else []
+        if number == chunks - 1:
+            waited = [*waited, *(piece for row in parts for piece in row)]
         last, exchanged = finish(number, 1, last, *waited)
         parts.append(exchanged)
     return project(info, weight_rows, held[1:], other, parts)

time: 226 us -> 226 us (level)
    ppermute x12, waiting for transfers between devices: 15.7 us -> 6.3 us  [swap_head(): return lax.ppermute(value, ('ctx', 'head'), pairs)]
    ppermute x16, waiting for transfers between devices: 16.3 us -> 23.9 us  [shift(): lax.ppermute(value, 'ctx', [(source, source + steps) for source in range(...]
    unnamed x55 -> x57, local copies, waits for them, and re-layouts: 9.5 us -> 9.34 us
  transfers between devices with their start and end apart: 33 -> 33, of which waited for: 11 -> 9; matrix products, arithmetic and copies ran while one was open for 4% -> 4% of each run, Pallas kernels for 46% -> 46%
where the time goes in v3:
time: 226 us; the launch traced here: 225 us
  Pallas kernels  122 us (54%)
  starting transfers between devices  57.3 us (25%)
  waiting for transfers between devices  30.2 us (13%)
  local copies, waits for them, and re-layouts  14.3 us (6%)
    pallas_call x4, Pallas kernels, attend_far(): kernel_call(functools.partial(far_body, places=len(queries), tile=tile, s...  61.4 us
    ppermute x16, starting transfers between devices, shift(): lax.ppermute(value, 'ctx', [(source, source + steps) for source in range(...  40.5 us
    ppermute x16, waiting for transfers between devices, shift(): lax.ppermute(value, 'ctx', [(source, source + steps) for source in range(...  23.9 us
    pallas_call x2, Pallas kernels, attend_local(): kernel_call(functools.partial(local_body, tile=tile, spots=spots), 'atten...  20.3 us
    ppermute x12, starting transfers between devices, swap_head(): return lax.ppermute(value, ('ctx', 'head'), pairs)  16 us
    pallas_call x1, Pallas kernels, project(): kernel_call(functools.partial(project_body, sources=sources, stages=stage...  14.3 us
    pallas_call x3, Pallas kernels, merge_local(): kernel_call(functools.partial(merge_local_body, heads=heads, runs=len(loc...  10.9 us
    pallas_call x4, Pallas kernels, merge_far(): kernel_call(functools.partial(merge_far_body, heads=heads, hops=hops), 'm...  10.7 us
  transfers between devices with their start and end apart: 33, of which 9 were waited for; matrix products, arithmetic and copies ran while one was open for 4% of the time, Pallas kernels for 46%

profile of v3, /device:TPU:0, one launch (start us, length us, event | category | flops | bytes accessed | tf_op | source)
XLA Modules:
  0.0 224.9 jit_solution(13000328325774812432)
XLA Ops:
  0.0 3.2 %fusion = (bf16[4,1,128,4,128]{4,3,2,1,0:T(4,128)(2,1)S(1)}, bf16[4,1,128,4,128]{4,3,2,1,0:T(4,128)(2,1)S(1)}, bf16[4,1,128,4,128]{4,3,2,1,0:T(4,128)(2,1)}, bf16[4,1,128,4,128]{4,3,2,1,0:T(4,128)(2,1)S(1)}) fusion(bf16[4,4,128,4,128]{4,3,2,1,0:T(4,128)(2,1)} %bitcast.36), kind=kLoop, calls=%fused_computation.9 | loop fusion | bytes 4194304 | tf_op jit(solution)/shard_map/slice | solution.py:622
  7.7 4.4 %prepare.1 = (bf16[4,144,2048]{2,1,0:T(8,128)(2,1)}, f32[4,16,128]{2,1,0:T(8,128)}, f32[4,16,128]{2,1,0:T(8,128)}, f32[4,16,128]{2,1,0:T(8,128)}) custom-call(s32[4]{0:T(128)} %pad_add_fusion.info_ref, bf16[2048,512]{1,0:T(8,128)(2,1)} %bitcast.42, s32[4,128,128]{2,1,0:T(8,128)} %pattern_ref.1), custom_call_target="tpu_custom_call" | custom-call | flops 4600000000 | bytes 1 | tf_op jit(solution)/shard_map/prepare/pallas_call | solution.py:80
  18.2 3.0 %collective-permute-done.refs_1_ = bf16[512,512]{1,0:T(8,128)(2,1)} collective-permute-done((bf16[512,512]{1,0:T(8,128)(2,1)}, bf16[512,512]{1,0:T(8,128)(2,1)}, u32[]{:S(2)}, u32[]{:S(2)}) %collective-permute-start) | collective-permute-done | bytes 524320 | tf_op jit(solution)/shard_map/ppermute | solution.py:586
  26.0 14.2 %attend_local.2 = (bf16[384,2048]{1,0:T(8,128)(2,1)}, bf16[3,16,2048]{2,1,0:T(8,128)(2,1)}) custom-call(bf16[2048,512]{1,0:T(8,128)(2,1)} %bitcast.40, bf16[2048,512]{1,0:T(8,128)(2,1)} %bitcast.30.key_ref.refs_3_, bf16[4,144,2048]{2,1,0:T(8,128)(2,1)} %get-tuple-element.56.value_ref.refs_5_, f32[4,16,128]{2,1,0:T(8,128)} %get-tuple-element.57.bias_ref), custom_call_target="tpu_custom_call" | custom-call | flops 11500000256 | bytes 1 | tf_op jit(solution)/shard_map/attend_local/pallas_call | solution.py:382
  40.3 4.1 %collective-permute-done.7.refs_2_ = bf16[512,512]{1,0:T(8,128)(2,1)} collective-permute-done((bf16[512,512]{1,0:T(8,128)(2,1)}, bf16[512,512]{1,0:T(8,128)(2,1)}, u32[]{:S(2)}, u32[]{:S(2)}) %collective-permute-start.7) | collective-permute-done | bytes 524320 | tf_op jit(solution)/shard_map/ppermute | solution.py:586
  45.7 2.0 collective-permute-start.2
  47.7 6.2 %attend_local.3 = (bf16[128,2048]{1,0:T(8,128)(2,1)}, bf16[1,16,2048]{2,1,0:T(8,128)(2,1)}) custom-call(bf16[2048,512]{1,0:T(8,128)(2,1)} %bitcast.41, bf16[2048,512]{1,0:T(8,128)(2,1)} %bitcast.30.key_ref.refs_3_, bf16[4,144,2048]{2,1,0:T(8,128)(2,1)} %get-tuple-element.56.value_ref.refs_5_, f32[4,16,128]{2,1,0:T(8,128)} %get-tuple-element.57.bias_ref), custom_call_target="tpu_custom_call" | custom-call | flops 11500000256 | bytes 1 | tf_op jit(solution)/shard_map/attend_local/pallas_call | solution.py:382
  53.9 6.1 %collective-permute-done.14.refs_1_ = bf16[512,512]{1,0:T(8,128)(2,1)} collective-permute-done((bf16[512,512]{1,0:T(8,128)(2,1)S(1)}, bf16[512,512]{1,0:T(8,128)(2,1)}, u32[]{:S(2)}, u32[]{:S(2)}) %collective-permute-start.14) | collective-permute-done | bytes 524320 | tf_op jit(solution)/shard_map/ppermute | solution.py:586
  64.1 15.4 %attend_far.4 = (bf16[528,512]{1,0:T(8,128)(2,1)}, bf16[528,512]{1,0:T(8,128)(2,1)}, bf16[528,512]{1,0:T(8,128)(2,1)}) custom-call(s32[4]{0:T(128)} %pad_add_fusion.info_ref, bf16[512,512]{1,0:T(8,128)(2,1)} %bitcast.35.refs_0_, bf16[512,512]{1,0:T(8,128)(2,1)} %collective-permute-done.refs_1_, bf16[512,512]{1,0:T(8,128)(2,1)} %collective-permute-done.7.refs_2_, ...), custom_call_target="tpu_custom_call" | custom-call | flops 18400000000 | bytes 1 | tf_op jit(solution)/shard_map/attend_far/pallas_call | solution.py:303
  79.5 6.6 %collective-permute-start.10 = (bf16[528,512]{1,0:T(8,128)(2,1)}, bf16[528,512]{1,0:T(8,128)(2,1)}, u32[]{:S(2)}, u32[]{:S(2)}) collective-permute-start(bf16[528,512]{1,0:T(8,128)(2,1)} %get-tuple-element.66), channel_id=1, source_target_pairs={{0,8},{4,12},{8,16},{12,20},{1,9},{5,13},{9,17},{13,21},{2,10},{6,... | collective-permute-start | bytes 1622024 | tf_op jit(solution)/shard_map/ppermute | solution.py:586
  86.9 15.3 %attend_far.5 = (bf16[528,512]{1,0:T(8,128)(2,1)}, bf16[528,512]{1,0:T(8,128)(2,1)}, bf16[528,512]{1,0:T(8,128)(2,1)}) custom-call(s32[4]{0:T(128)} %pad_add_fusion.info_ref, bf16[512,512]{1,0:T(8,128)(2,1)} %bitcast.34.refs_0_, bf16[512,512]{1,0:T(8,128)(2,1)} %collective-permute-done.11.refs_1_, bf16[512,512]{1,0:T(8,128)(2,1)} %copy-done.15, ...), custom_call_target="tpu_custom_call" | custom-call | flops 18400000000 | bytes 1 | tf_op jit(solution)/shard_map/attend_far/pallas_call | solution.py:303
  102.3 3.9 %collective-permute-start.19 = (bf16[528,512]{1,0:T(8,128)(2,1)}, bf16[528,512]{1,0:T(8,128)(2,1)S(1)}, u32[]{:S(2)}, u32[]{:S(2)}) collective-permute-start(bf16[528,512]{1,0:T(8,128)(2,1)} %get-tuple-element.69), channel_id=1, source_target_pairs={{0,8},{4,12},{8,16},{12,20},{1,9},{5,13},{9,17},{13,21},{2,10},{6,... | collective-permute-start | bytes 1622024 | tf_op jit(solution)/shard_map/ppermute | solution.py:586
  109.3 2.6 %merge_far.4 = bf16[528,512]{1,0:T(8,128)(2,1)} custom-call(s32[4]{0:T(128)} %pad_add_fusion.info_ref, bf16[528,512]{1,0:T(8,128)(2,1)} %collective-permute-done.10.refs_0_, bf16[528,512]{1,0:T(8,128)(2,1)} %get-tuple-element.71.refs_1_.refs_5_, bf16[528,512]{1,0:T(8,128)(2,1)} %get-tuple-element.72.refs_2_.refs_6_), custom_call_target="tpu_custom_call" | custom-call | flops 46000001024 | bytes 1 | tf_op jit(solution)/shard_map/merge_far/pallas_call | solution.py:447
  111.9 4.6 %collective-permute-start.13 = (bf16[528,512]{1,0:T(8,128)(2,1)}, bf16[528,512]{1,0:T(8,128)(2,1)S(1)}, u32[]{:S(2)}, u32[]{:S(2)}) collective-permute-start(bf16[528,512]{1,0:T(8,128)(2,1)} %merge_far.4), channel_id=1, source_target_pairs={{0,8},{4,12},{8,16},{12,20},{16,24},{20,28},{1,9},{5,13},{9,17},{1... | collective-permute-start | bytes 1622024 | tf_op jit(solution)/shard_map/ppermute | solution.py:586
  116.5 15.3 %attend_far.6 = (bf16[528,512]{1,0:T(8,128)(2,1)}, bf16[528,512]{1,0:T(8,128)(2,1)}, bf16[528,512]{1,0:T(8,128)(2,1)}) custom-call(s32[4]{0:T(128)} %pad_add_fusion.info_ref, bf16[512,512]{1,0:T(8,128)(2,1)} %bitcast.52, bf16[512,512]{1,0:T(8,128)(2,1)} %collective-permute-done.14.refs_1_, bf16[512,512]{1,0:T(8,128)(2,1)} %collective-permute-done.15.refs_2_, ...), custom_call_target="tpu_custom_call" | custom-call | flops 18400000000 | bytes 1 | tf_op jit(solution)/shard_map/attend_far/pallas_call | solution.py:303
  131.9 3.0 %collective-permute-start.16 = (bf16[528,512]{1,0:T(8,128)(2,1)}, bf16[528,512]{1,0:T(8,128)(2,1)}, u32[]{:S(2)}, u32[]{:S(2)}) collective-permute-start(bf16[528,512]{1,0:T(8,128)(2,1)} %get-tuple-element.76), channel_id=1, source_target_pairs={{0,8},{4,12},{8,16},{12,20},{1,9},{5,13},{9,17},{13,21},{2,10},{6,... | collective-permute-start | bytes 1622024 | tf_op jit(solution)/shard_map/ppermute | solution.py:586
  135.0 2.6 %merge_far.5 = bf16[528,512]{1,0:T(8,128)(2,1)} custom-call(s32[4]{0:T(128)} %pad_add_fusion.info_ref, bf16[528,512]{1,0:T(8,128)(2,1)} %copy-done.11, bf16[528,512]{1,0:T(8,128)(2,1)} %get-tuple-element.80.refs_1_.refs_8_, bf16[528,512]{1,0:T(8,128)(2,1)} %get-tuple-element.81.refs_2_.refs_9_), custom_call_target="tpu_custom_call" | custom-call | flops 46000001024 | bytes 1 | tf_op jit(solution)/shard_map/merge_far/pallas_call | solution.py:447
  139.0 15.4 %attend_far.7 = (bf16[528,512]{1,0:T(8,128)(2,1)}, bf16[528,512]{1,0:T(8,128)(2,1)}, bf16[528,512]{1,0:T(8,128)(2,1)}) custom-call(s32[4]{0:T(128)} %pad_add_fusion.info_ref, bf16[512,512]{1,0:T(8,128)(2,1)} %bitcast.50, bf16[512,512]{1,0:T(8,128)(2,1)} %collective-permute-done.17.refs_1_, bf16[512,512]{1,0:T(8,128)(2,1)} %copy-done.14, ...), custom_call_target="tpu_custom_call" | custom-call | flops 18400000000 | bytes 1 | tf_op jit(solution)/shard_map/attend_far/pallas_call | solution.py:303
  156.1 2.5 %collective-permute-done.20.refs_7_ = bf16[528,512]{1,0:T(8,128)(2,1)S(1)} collective-permute-done((bf16[528,512]{1,0:T(8,128)(2,1)}, bf16[528,512]{1,0:T(8,128)(2,1)S(1)}, u32[]{:S(2)}, u32[]{:S(2)}) %collective-permute-start.20) | collective-permute-done | bytes 540704 | tf_op jit(solution)/shard_map/ppermute | solution.py:586
  158.6 2.8 %merge_far.6 = bf16[528,512]{1,0:T(8,128)(2,1)} custom-call(s32[4]{0:T(128)} %pad_add_fusion.info_ref, bf16[528,512]{1,0:T(8,128)(2,1)} %collective-permute-done.16.refs_0_, bf16[528,512]{1,0:T(8,128)(2,1)} %get-tuple-element.85.refs_1_.refs_5_, bf16[528,512]{1,0:T(8,128)(2,1)} %get-tuple-element.86.refs_2_.refs_6_), custom_call_target="tpu_custom_call" | custom-call | flops 46000001024 | bytes 1 | tf_op jit(solution)/shard_map/merge_far/pallas_call | solution.py:447
  161.5 4.5 %collective-permute-start.24 = (bf16[528,512]{1,0:T(8,128)(2,1)}, bf16[528,512]{1,0:T(8,128)(2,1)S(1)}, u32[]{:S(2)}, u32[]{:S(2)}) collective-permute-start(bf16[528,512]{1,0:T(8,128)(2,1)} %merge_far.6), channel_id=1, source_target_pairs={{0,8},{4,12},{8,16},{12,20},{16,24},{20,28},{1,9},{5,13},{9,17},{1... | collective-permute-start | bytes 1622024 | tf_op jit(solution)/shard_map/ppermute | solution.py:586
  166.0 4.7 %merge_local.3 = (bf16[256,512]{1,0:T(8,128)(2,1)}, bf16[256,512]{1,0:T(8,128)(2,1)}, bf16[256,512]{1,0:T(8,128)(2,1)}, bf16[256,512]{1,0:T(8,128)(2,1)}) custom-call(s32[4]{0:T(128)} %pad_add_fusion.info_ref, bf16[384,2048]{1,0:T(8,128)(2,1)} %get-tuple-element.58.refs_0_, bf16[3,16,2048]{2,1,0:T(8,128)(2,1)} %get-tuple-element.59.refs_1_, ...), custom_call_target="tpu_custom_call" | custom-call | flops 46000001024 | bytes 1 | tf_op jit(solution)/shard_map/merge_local/pallas_call | solution.py:497
  172.9 2.6 %merge_far.7 = bf16[528,512]{1,0:T(8,128)(2,1)} custom-call(s32[4]{0:T(128)} %pad_add_fusion.info_ref, bf16[528,512]{1,0:T(8,128)(2,1)} %copy-done.13, bf16[528,512]{1,0:T(8,128)(2,1)} %get-tuple-element.93.refs_1_.refs_5_, bf16[528,512]{1,0:T(8,128)(2,1)} %get-tuple-element.94.refs_2_.refs_6_), custom_call_target="tpu_custom_call" | custom-call | flops 46000001024 | bytes 1 | tf_op jit(solution)/shard_map/merge_far/pallas_call | solution.py:447
  177.6 3.5 %collective-permute-done.24.refs_4_ = bf16[528,512]{1,0:T(8,128)(2,1)S(1)} collective-permute-done((bf16[528,512]{1,0:T(8,128)(2,1)}, bf16[528,512]{1,0:T(8,128)(2,1)S(1)}, u32[]{:S(2)}, u32[]{:S(2)}) %collective-permute-start.24) | collective-permute-done | bytes 540704 | tf_op jit(solution)/shard_map/ppermute | solution.py:586
  181.0 4.3 %collective-permute-start.29 = (bf16[528,512]{1,0:T(8,128)(2,1)}, bf16[528,512]{1,0:T(8,128)(2,1)S(1)}, u32[]{:S(2)}, u32[]{:S(2)}) collective-permute-start(bf16[528,512]{1,0:T(8,128)(2,1)} %merge_far.7), channel_id=1, source_target_pairs={{0,8},{4,12},{8,16},{12,20},{16,24},{20,28},{1,9},{5,13},{9,17},{1... | collective-permute-start | bytes 1622024 | tf_op jit(solution)/shard_map/ppermute | solution.py:586
  185.4 3.1 %merge_local.4 = (bf16[128,512]{1,0:T(8,128)(2,1)}, bf16[128,512]{1,0:T(8,128)(2,1)}, bf16[128,512]{1,0:T(8,128)(2,1)}, bf16[128,512]{1,0:T(8,128)(2,1)}) custom-call(s32[4]{0:T(128)} %pad_add_fusion.info_ref, bf16[384,2048]{1,0:T(8,128)(2,1)} %get-tuple-element.58.refs_0_, bf16[3,16,2048]{2,1,0:T(8,128)(2,1)} %get-tuple-element.59.refs_1_, ...), custom_call_target="tpu_custom_call" | custom-call | flops 46000001024 | bytes 1 | tf_op jit(solution)/shard_map/merge_local/pallas_call | solution.py:497
  192.0 4.7 %collective-permute-done.29.refs_4_ = bf16[528,512]{1,0:T(8,128)(2,1)S(1)} collective-permute-done((bf16[528,512]{1,0:T(8,128)(2,1)}, bf16[528,512]{1,0:T(8,128)(2,1)S(1)}, u32[]{:S(2)}, u32[]{:S(2)}) %collective-permute-start.29) | collective-permute-done | bytes 540704 | tf_op jit(solution)/shard_map/ppermute | solution.py:586
  197.9 3.2 %merge_local.5 = (bf16[128,512]{1,0:T(8,128)(2,1)}, bf16[128,512]{1,0:T(8,128)(2,1)}, bf16[128,512]{1,0:T(8,128)(2,1)}, bf16[128,512]{1,0:T(8,128)(2,1)}) custom-call(s32[4]{0:T(128)} %pad_add_fusion.info_ref, bf16[384,2048]{1,0:T(8,128)(2,1)} %get-tuple-element.58.refs_0_, bf16[3,16,2048]{2,1,0:T(8,128)(2,1)} %get-tuple-element.59.refs_1_, ...), custom_call_target="tpu_custom_call" | custom-call | flops 46000001024 | bytes 1 | tf_op jit(solution)/shard_map/merge_local/pallas_call | solution.py:497
  202.6 2.1 collective-permute-start.32
  204.7 3.0 %collective-permute-done.30.refs_15_ = bf16[128,512]{1,0:T(8,128)(2,1)S(1)} collective-permute-done((bf16[128,512]{1,0:T(8,128)(2,1)}, bf16[128,512]{1,0:T(8,128)(2,1)S(1)}, u32[]{:S(2)}, u32[]{:S(2)}) %collective-permute-start.30) | collective-permute-done | bytes 131104 | tf_op jit(solution)/shard_map/ppermute | solution.py:599
  207.7 2.0 collective-permute-done.31.refs_16_
  210.4 14.3 %project.1 = bf16[512,4096]{1,0:T(8,128)(2,1)} custom-call(s32[4]{0:T(128)} %pad_add_fusion.info_ref, bf16[512,4096]{1,0:T(8,128)(2,1)} %bitcast.48, bf16[256,4096]{1,0:T(8,128)(2,1)} %collective-permute-done.1.refs_0_, bf16[256,4096]{1,0:T(8,128)(2,1)} %collective-permute-done.2.refs_1_, bf16[256,4096]{1,0:T(8,128)(2,1)} %copy-done.7, ...), custom_call_target="tpu_custom_call" | custom-call | flops 17250000896 | bytes 1 | tf_op jit(solution)/shard_map/project/pallas_call | solution.py:567
  (109 shorter events, 39.1 us)
Async XLA Ops:
  4.1 17.2 %collective-permute-start = (bf16[512,512]{1,0:T(8,128)(2,1)}, bf16[512,512]{1,0:T(8,128)(2,1)}, u32[]{:S(2)}, u32[]{:S(2)}) collective-permute-start(bf16[512,512]{1,0:T(8,128)(2,1)} %bitcast.35.refs_0_), channel_id=1, source_target_pairs={{8,0},{12,4},{16,8},{20,12},{24,16},{28,20},{9,1},{13,5},{17,9},{2... | collective-permute-start | bytes 1572872 | tf_op jit(solution)/shard_map/ppermute | solution.py:586
  12.0 52.1 %collective-permute-start.9 = (bf16[4,144,2048]{2,1,0:T(8,128)(2,1)}, bf16[4,144,2048]{2,1,0:T(8,128)(2,1)}, u32[]{:S(2)}, u32[]{:S(2)}) collective-permute-start(bf16[4,144,2048]{2,1,0:T(8,128)(2,1)} %get-tuple-element.56.value_ref.refs_5_), channel_id=1, source_target_pairs={{0,4},{4,0},{8,12},{12,8},{16,20},{20,16},{24,28},{28,24},{1,5},{5... | collective-permute-start | bytes 7077896 | tf_op jit(solution)/shard_map/ppermute | solution.py:590
  14.2 48.4 %collective-permute-start.8 = (bf16[2048,512]{1,0:T(8,128)(2,1)}, bf16[2048,512]{1,0:T(8,128)(2,1)}, u32[]{:S(2)}, u32[]{:S(2)}) collective-permute-start(bf16[2048,512]{1,0:T(8,128)(2,1)} %bitcast.30.key_ref.refs_3_), channel_id=1, source_target_pairs={{0,4},{4,0},{8,12},{12,8},{16,20},{20,16},{24,28},{28,24},{1,5},{5... | collective-permute-start | bytes 6291464 | tf_op jit(solution)/shard_map/ppermute | solution.py:590
  15.2 30.5 %collective-permute-start.11 = (bf16[512,512]{1,0:T(8,128)(2,1)}, bf16[512,512]{1,0:T(8,128)(2,1)}, u32[]{:S(2)}, u32[]{:S(2)}) collective-permute-start(bf16[512,512]{1,0:T(8,128)(2,1)} %bitcast.34.refs_0_), channel_id=1, source_target_pairs={{8,0},{12,4},{16,8},{20,12},{24,16},{28,20},{9,1},{13,5},{17,9},{2... | collective-permute-start | bytes 1572872 | tf_op jit(solution)/shard_map/ppermute | solution.py:586
  21.2 23.2 %collective-permute-start.7 = (bf16[512,512]{1,0:T(8,128)(2,1)}, bf16[512,512]{1,0:T(8,128)(2,1)}, u32[]{:S(2)}, u32[]{:S(2)}) collective-permute-start(bf16[512,512]{1,0:T(8,128)(2,1)} %collective-permute-done.refs_1_), channel_id=1, source_target_pairs={{8,0},{12,4},{16,8},{20,12},{9,1},{13,5},{17,9},{21,13},{10,2},{14... | collective-permute-start | bytes 1572872 | tf_op jit(solution)/shard_map/ppermute | solution.py:586
  24.3 37.0 %collective-permute-start.1 = (bf16[256,4096]{1,0:T(8,128)(2,1)S(1)}, bf16[256,4096]{1,0:T(8,128)(2,1)}, u32[]{:S(2)}, u32[]{:S(2)}) collective-permute-start(bf16[256,4096]{1,0:T(8,128)(2,1)S(1)} %constant_dynamic-slice_fusion), channel_id=1, source_target_pairs={{0,1},{1,0},{2,3},{3,2},{4,6},{5,7},{6,4},{7,5},{8,9},{9,8},{10,11... | collective-permute-start | bytes 6291464 | tf_op jit(solution)/shard_map/ppermute | solution.py:599
  44.4 15.6 %collective-permute-start.14 = (bf16[512,512]{1,0:T(8,128)(2,1)S(1)}, bf16[512,512]{1,0:T(8,128)(2,1)}, u32[]{:S(2)}, u32[]{:S(2)}) collective-permute-start(bf16[512,512]{1,0:T(8,128)(2,1)S(1)} %bitcast.51), channel_id=1, source_target_pairs={{8,0},{12,4},{16,8},{20,12},{24,16},{28,20},{9,1},{13,5},{17,9},{2... | collective-permute-start | bytes 1572872 | tf_op jit(solution)/shard_map/ppermute | solution.py:586
  45.7 40.4 %collective-permute-start.2 = (bf16[256,4096]{1,0:T(8,128)(2,1)S(1)}, bf16[256,4096]{1,0:T(8,128)(2,1)}, u32[]{:S(2)}, u32[]{:S(2)}) collective-permute-start(bf16[256,4096]{1,0:T(8,128)(2,1)S(1)} %constant_dynamic-slice_fusion), channel_id=1, source_target_pairs={{0,2},{1,3},{2,0},{3,1},{4,5},{5,4},{6,7},{7,6},{8,10},{9,11},{10,... | collective-permute-start | bytes 6291464 | tf_op jit(solution)/shard_map/ppermute | solution.py:599
  60.0 26.1 %collective-permute-start.12 = (bf16[512,512]{1,0:T(8,128)(2,1)}, bf16[512,512]{1,0:T(8,128)(2,1)S(1)}, u32[]{:S(2)}, u32[]{:S(2)}) collective-permute-start(bf16[512,512]{1,0:T(8,128)(2,1)} %collective-permute-done.11.refs_1_), channel_id=1, source_target_pairs={{8,0},{12,4},{16,8},{20,12},{9,1},{13,5},{17,9},{21,13},{10,2},{14... | collective-permute-start | bytes 1572872 | tf_op jit(solution)/shard_map/ppermute | solution.py:586
  61.3 50.6 %collective-permute-start.15 = (bf16[512,512]{1,0:T(8,128)(2,1)}, bf16[512,512]{1,0:T(8,128)(2,1)}, u32[]{:S(2)}, u32[]{:S(2)}) collective-permute-start(bf16[512,512]{1,0:T(8,128)(2,1)} %collective-permute-done.14.refs_1_), channel_id=1, source_target_pairs={{8,0},{12,4},{16,8},{20,12},{9,1},{13,5},{17,9},{21,13},{10,2},{14... | collective-permute-start | bytes 1572872 | tf_op jit(solution)/shard_map/ppermute | solution.py:586
  62.6 43.6 %collective-permute-start.17 = (bf16[512,512]{1,0:T(8,128)(2,1)S(1)}, bf16[512,512]{1,0:T(8,128)(2,1)}, u32[]{:S(2)}, u32[]{:S(2)}) collective-permute-start(bf16[512,512]{1,0:T(8,128)(2,1)S(1)} %bitcast.49), channel_id=1, source_target_pairs={{8,0},{12,4},{16,8},{20,12},{24,16},{28,20},{9,1},{13,5},{17,9},{2... | collective-permute-start | bytes 1572872 | tf_op jit(solution)/shard_map/ppermute | solution.py:586
  79.5 29.8 %collective-permute-start.10 = (bf16[528,512]{1,0:T(8,128)(2,1)}, bf16[528,512]{1,0:T(8,128)(2,1)}, u32[]{:S(2)}, u32[]{:S(2)}) collective-permute-start(bf16[528,512]{1,0:T(8,128)(2,1)} %get-tuple-element.66), channel_id=1, source_target_pairs={{0,8},{4,12},{8,16},{12,20},{1,9},{5,13},{9,17},{13,21},{2,10},{6,... | collective-permute-start | bytes 1622024 | tf_op jit(solution)/shard_map/ppermute | solution.py:586
  102.3 29.5 %collective-permute-start.19 = (bf16[528,512]{1,0:T(8,128)(2,1)}, bf16[528,512]{1,0:T(8,128)(2,1)S(1)}, u32[]{:S(2)}, u32[]{:S(2)}) collective-permute-start(bf16[528,512]{1,0:T(8,128)(2,1)} %get-tuple-element.69), channel_id=1, source_target_pairs={{0,8},{4,12},{8,16},{12,20},{1,9},{5,13},{9,17},{13,21},{2,10},{6,... | collective-permute-start | bytes 1622024 | tf_op jit(solution)/shard_map/ppermute | solution.py:586
  106.2 31.4 %collective-permute-start.18 = (bf16[512,512]{1,0:T(8,128)(2,1)}, bf16[512,512]{1,0:T(8,128)(2,1)S(1)}, u32[]{:S(2)}, u32[]{:S(2)}) collective-permute-start(bf16[512,512]{1,0:T(8,128)(2,1)} %collective-permute-done.17.refs_1_), channel_id=1, source_target_pairs={{8,0},{12,4},{16,8},{20,12},{9,1},{13,5},{17,9},{21,13},{10,2},{14... | collective-permute-start | bytes 1572872 | tf_op jit(solution)/shard_map/ppermute | solution.py:586
  107.5 31.4 %collective-permute-start.3 = (bf16[256,4096]{1,0:T(8,128)(2,1)}, bf16[256,4096]{1,0:T(8,128)(2,1)S(1)}, u32[]{:S(2)}, u32[]{:S(2)}) collective-permute-start(bf16[256,4096]{1,0:T(8,128)(2,1)} %collective-permute-done.1.refs_0_), channel_id=1, source_target_pairs={{0,2},{1,3},{2,0},{3,1},{4,5},{5,4},{6,7},{7,6},{8,10},{9,11},{10,... | collective-permute-start | bytes 6291464 | tf_op jit(solution)/shard_map/ppermute | solution.py:599
  109.3 66.3 %collective-permute-start.4 = (bf16[256,4096]{1,0:T(8,128)(2,1)}, bf16[256,4096]{1,0:T(8,128)(2,1)}, u32[]{:S(2)}, u32[]{:S(2)}) collective-permute-start(bf16[256,4096]{1,0:T(8,128)(2,1)} %collective-permute-done.1.refs_0_), channel_id=1, source_target_pairs={{0,4},{4,0},{8,12},{12,8},{16,20},{20,16},{24,28},{28,24},{1,5},{5... | collective-permute-start | bytes 6291464 | tf_op jit(solution)/shard_map/ppermute | solution.py:590
  111.9 20.0 %collective-permute-start.13 = (bf16[528,512]{1,0:T(8,128)(2,1)}, bf16[528,512]{1,0:T(8,128)(2,1)S(1)}, u32[]{:S(2)}, u32[]{:S(2)}) collective-permute-start(bf16[528,512]{1,0:T(8,128)(2,1)} %merge_far.4), channel_id=1, source_target_pairs={{0,8},{4,12},{8,16},{12,20},{16,24},{20,28},{1,9},{5,13},{9,17},{1... | collective-permute-start | bytes 1622024 | tf_op jit(solution)/shard_map/ppermute | solution.py:586
  131.8 44.3 %collective-permute-start.5 = (bf16[256,4096]{1,0:T(8,128)(2,1)}, bf16[256,4096]{1,0:T(8,128)(2,1)}, u32[]{:S(2)}, u32[]{:S(2)}) collective-permute-start(bf16[256,4096]{1,0:T(8,128)(2,1)} %collective-permute-done.2.refs_1_), channel_id=1, source_target_pairs={{0,4},{4,0},{8,12},{12,8},{16,20},{20,16},{24,28},{28,24},{1,5},{5... | collective-permute-start | bytes 6291464 | tf_op jit(solution)/shard_map/ppermute | solution.py:590
  131.9 24.1 %collective-permute-start.16 = (bf16[528,512]{1,0:T(8,128)(2,1)}, bf16[528,512]{1,0:T(8,128)(2,1)}, u32[]{:S(2)}, u32[]{:S(2)}) collective-permute-start(bf16[528,512]{1,0:T(8,128)(2,1)} %get-tuple-element.76), channel_id=1, source_target_pairs={{0,8},{4,12},{8,16},{12,20},{1,9},{5,13},{9,17},{13,21},{2,10},{6,... | collective-permute-start | bytes 1622024 | tf_op jit(solution)/shard_map/ppermute | solution.py:586
  137.6 21.0 %collective-permute-start.20 = (bf16[528,512]{1,0:T(8,128)(2,1)}, bf16[528,512]{1,0:T(8,128)(2,1)S(1)}, u32[]{:S(2)}, u32[]{:S(2)}) collective-permute-start(bf16[528,512]{1,0:T(8,128)(2,1)} %merge_far.5), channel_id=1, source_target_pairs={{0,8},{4,12},{8,16},{12,20},{16,24},{20,28},{1,9},{5,13},{9,17},{1... | collective-permute-start | bytes 1622024 | tf_op jit(solution)/shard_map/ppermute | solution.py:586
  154.4 17.8 %collective-permute-start.25 = (bf16[528,512]{1,0:T(8,128)(2,1)}, bf16[528,512]{1,0:T(8,128)(2,1)S(1)}, u32[]{:S(2)}, u32[]{:S(2)}) collective-permute-start(bf16[528,512]{1,0:T(8,128)(2,1)} %get-tuple-element.83), channel_id=1, source_target_pairs={{0,8},{4,12},{8,16},{12,20},{1,9},{5,13},{9,17},{13,21},{2,10},{6,... | collective-permute-start | bytes 1622024 | tf_op jit(solution)/shard_map/ppermute | solution.py:586
  161.5 19.6 %collective-permute-start.24 = (bf16[528,512]{1,0:T(8,128)(2,1)}, bf16[528,512]{1,0:T(8,128)(2,1)S(1)}, u32[]{:S(2)}, u32[]{:S(2)}) collective-permute-start(bf16[528,512]{1,0:T(8,128)(2,1)} %merge_far.6), channel_id=1, source_target_pairs={{0,8},{4,12},{8,16},{12,20},{16,24},{20,28},{1,9},{5,13},{9,17},{1... | collective-permute-start | bytes 1622024 | tf_op jit(solution)/shard_map/ppermute | solution.py:586
  170.7 19.3 %collective-permute-start.21 = (bf16[256,512]{1,0:T(8,128)(2,1)}, bf16[256,512]{1,0:T(8,128)(2,1)S(1)}, u32[]{:S(2)}, u32[]{:S(2)}) collective-permute-start(bf16[256,512]{1,0:T(8,128)(2,1)} %get-tuple-element.89), channel_id=1, source_target_pairs={{0,1},{1,0},{2,3},{3,2},{4,6},{5,7},{6,4},{7,5},{8,9},{9,8},{10,11... | collective-permute-start | bytes 786440 | tf_op jit(solution)/shard_map/ppermute | solution.py:599
  172.2 13.2 %collective-permute-start.6 = (bf16[256,4096]{1,0:T(8,128)(2,1)S(1)}, bf16[256,4096]{1,0:T(8,128)(2,1)}, u32[]{:S(2)}, u32[]{:S(2)}) collective-permute-start(bf16[256,4096]{1,0:T(8,128)(2,1)S(1)} %collective-permute-done.3.refs_2_), channel_id=1, source_target_pairs={{0,4},{4,0},{8,12},{12,8},{16,20},{20,16},{24,28},{28,24},{1,5},{5... | collective-permute-start | bytes 6291464 | tf_op jit(solution)/shard_map/ppermute | solution.py:590
  175.6 14.9 %collective-permute-start.22 = (bf16[256,512]{1,0:T(8,128)(2,1)}, bf16[256,512]{1,0:T(8,128)(2,1)S(1)}, u32[]{:S(2)}, u32[]{:S(2)}) collective-permute-start(bf16[256,512]{1,0:T(8,128)(2,1)} %get-tuple-element.90), channel_id=1, source_target_pairs={{0,2},{1,3},{2,0},{3,1},{4,5},{5,4},{6,7},{7,6},{8,10},{9,11},{10,... | collective-permute-start | bytes 786440 | tf_op jit(solution)/shard_map/ppermute | solution.py:599
  176.1 15.9 %collective-permute-start.23 = (bf16[256,512]{1,0:T(8,128)(2,1)}, bf16[256,512]{1,0:T(8,128)(2,1)S(1)}, u32[]{:S(2)}, u32[]{:S(2)}) collective-permute-start(bf16[256,512]{1,0:T(8,128)(2,1)} %get-tuple-element.91), channel_id=1, source_target_pairs={{0,3},{1,2},{2,1},{3,0},{4,7},{5,6},{6,5},{7,4},{8,11},{9,10},{10,... | collective-permute-start | bytes 786440 | tf_op jit(solution)/shard_map/ppermute | solution.py:599
  181.0 15.6 %collective-permute-start.29 = (bf16[528,512]{1,0:T(8,128)(2,1)}, bf16[528,512]{1,0:T(8,128)(2,1)S(1)}, u32[]{:S(2)}, u32[]{:S(2)}) collective-permute-start(bf16[528,512]{1,0:T(8,128)(2,1)} %merge_far.7), channel_id=1, source_target_pairs={{0,8},{4,12},{8,16},{12,20},{16,24},{20,28},{1,9},{5,13},{9,17},{1... | collective-permute-start | bytes 1622024 | tf_op jit(solution)/shard_map/ppermute | solution.py:586
  188.4 8.2 %collective-permute-start.26 = (bf16[128,512]{1,0:T(8,128)(2,1)}, bf16[128,512]{1,0:T(8,128)(2,1)S(1)}, u32[]{:S(2)}, u32[]{:S(2)}) collective-permute-start(bf16[128,512]{1,0:T(8,128)(2,1)} %get-tuple-element.97), channel_id=1, source_target_pairs={{0,1},{1,0},{2,3},{3,2},{4,6},{5,7},{6,4},{7,5},{8,9},{9,8},{10,11... | collective-permute-start | bytes 393224 | tf_op jit(solution)/shard_map/ppermute | solution.py:599
  189.9 8.0 %collective-permute-start.27 = (bf16[128,512]{1,0:T(8,128)(2,1)}, bf16[128,512]{1,0:T(8,128)(2,1)S(1)}, u32[]{:S(2)}, u32[]{:S(2)}) collective-permute-start(bf16[128,512]{1,0:T(8,128)(2,1)} %get-tuple-element.98), channel_id=1, source_target_pairs={{0,2},{1,3},{2,0},{3,1},{4,5},{5,4},{6,7},{7,6},{8,10},{9,11},{10,... | collective-permute-start | bytes 393224 | tf_op jit(solution)/shard_map/ppermute | solution.py:599
  190.4 7.5 %collective-permute-start.28 = (bf16[128,512]{1,0:T(8,128)(2,1)}, bf16[128,512]{1,0:T(8,128)(2,1)S(1)}, u32[]{:S(2)}, u32[]{:S(2)}) collective-permute-start(bf16[128,512]{1,0:T(8,128)(2,1)} %get-tuple-element.99), channel_id=1, source_target_pairs={{0,3},{1,2},{2,1},{3,0},{4,7},{5,6},{6,5},{7,4},{8,11},{9,10},{10,... | collective-permute-start | bytes 393224 | tf_op jit(solution)/shard_map/ppermute | solution.py:599
  202.1 7.6 %collective-permute-start.31 = (bf16[128,512]{1,0:T(8,128)(2,1)}, bf16[128,512]{1,0:T(8,128)(2,1)S(1)}, u32[]{:S(2)}, u32[]{:S(2)}) collective-permute-start(bf16[128,512]{1,0:T(8,128)(2,1)} %get-tuple-element.103), channel_id=1, source_target_pairs={{0,2},{1,3},{2,0},{3,1},{4,5},{5,4},{6,7},{7,6},{8,10},{9,11},{10,... | collective-permute-start | bytes 393224 | tf_op jit(solution)/shard_map/ppermute | solution.py:599
  202.6 7.1 %collective-permute-start.32 = (bf16[128,512]{1,0:T(8,128)(2,1)}, bf16[128,512]{1,0:T(8,128)(2,1)S(1)}, u32[]{:S(2)}, u32[]{:S(2)}) collective-permute-start(bf16[128,512]{1,0:T(8,128)(2,1)} %get-tuple-element.104), channel_id=1, source_target_pairs={{0,3},{1,2},{2,1},{3,0},{4,7},{5,6},{6,5},{7,4},{8,11},{9,10},{10,... | collective-permute-start | bytes 393224 | tf_op jit(solution)/shard_map/ppermute | solution.py:599
  (26 other events, 158.9 us)
